TPU v7x, 256 devices: a whole 4x4x8 slice. The times are simulated.
256 devices in a mesh: row: 32 (over y, z), col: 8 (over x, core).
Axes of the slice: x: 4, y: 4, z: 8, core: 2. Of those that a mesh axis runs over, the one named last changes fastest.
Arguments:
- rhs: float32 [32, 524288], P(None, ('row', 'col')), may hold values from -5 to 7
- coords: float32 [3, 524288], P(None, ('row', 'col')), may hold values from 0 to 16, as said below
- nugget: float32 [524288], P(('row', 'col')), may hold values from 1.5 to 3
- near_ids: int32 [1024, 3], P(('row', 'col')), may hold values from -1 to 1023, as said below
- basis: float32 [10, 128, 524288], P(None, None, ('row', 'col')), may hold values from -6 to 6
Outputs:
- solution: float32 [32, 524288], P(None, ('row', 'col'))
- residual: float32 [32, 524288], P(None, ('row', 'col'))
Inputs may be any that keep to these rules, and one draw needn't show every extreme that they name: `near_ids`: row i lists leaf i and some of the leaves i - 1 to i + 1 inside the range, each at most once, in any order; the other slots hold -1; the first and last leaf of each device's block of 4 list all such leaves inside the range. `coords`: each leaf's points lie in a unit box with an integer corner; consecutive leaves lie in boxes that share a face.
All inputs are finite; a program needn't handle non-finite values.
Results may differ from a plain program's by a relative error of at most 0.0003.
Values sent between devices are 32-bit elements; how exact they have to be, the bound alone decides.
A program may use at most 128 MiB of HBM per device.

v0:
```python
import jax
import jax.numpy as jnp
from jax import lax
from jax.sharding import PartitionSpec as P

LEAF = 512
ITERS = 4
REACH = 1
WIN = 3


root_three = 1.7320508075688772
spacing_factor = 1.6


def padded(cells, sides, width):
    for axis, dim in sides:
        count = lax.axis_size(axis)
        ends = count - 1
        head = lax.slice_in_dim(cells, 0, width, axis=dim)
        tail = lax.slice_in_dim(cells, cells.shape[dim] - width, cells.shape[dim], axis=dim)
        cells = jnp.concatenate(
            [
                lax.ppermute(tail, axis, [(i, (i + 1) % count) for i in range(ends)]),
                cells,
                lax.ppermute(head, axis, [((i + 1) % count, i) for i in range(ends)]),
            ],
            axis=dim,
        )
    return cells


def partner(value, axis, stride):
    mask = 2**stride
    pairs = [(source, source ^ mask) for source in range(lax.axis_size(axis))]
    return lax.ppermute(value, axis, pairs)


def matern(square_dist):
    length = spacing_factor * LEAF ** (-1.0 / 3.0)
    scaled = root_three * jnp.sqrt(square_dist) / length
    return (1.0 + scaled) * jnp.exp(-scaled)


def window_mask(near_ids, first_leaf, count):
    leaves = first_leaf + jnp.arange(count, dtype=jnp.int32)
    offsets = jnp.arange(WIN, dtype=jnp.int32) - REACH
    target = leaves[None, :] + offsets[:, None]
    matches = near_ids.T[None, :, :] == target[:, None, :]
    return jnp.any(matches, axis=1).astype(jnp.float32)


def tile_block(own_coords, far_coords, weight):
    spread = own_coords[:, :, :, None] - far_coords[:, :, None, :]
    square_dist = jnp.sum(spread * spread, axis=0)
    return matern(square_dist) * (weight / (16 * WIN))[:, None, None]


def per_device(rhs, coords, nugget, near_ids, basis):
    width = rhs.shape[1]
    leaves = width // LEAF
    levels = basis.shape[0]
    leaf_bits = leaves.bit_length() - 1
    col_bits = lax.axis_size("col").bit_length() - 1
    mask = window_mask(near_ids, lax.axis_index(("row", "col")) * leaves, leaves)
    coord_halo = padded(coords, ((("row", "col"), 1),), REACH * LEAF)
    own = coords.reshape(3, leaves, LEAF)

    def build_tiles():
        return [
            tile_block(
                own,
                coord_halo[:, offset * LEAF : offset * LEAF + width].reshape(3, leaves, LEAF),
                mask[offset],
            )
            for offset in range(WIN)
        ]

    def near_field(field):
        tile_list = build_tiles()
        field_halo = padded(field, ((("row", "col"), 1),), REACH * LEAF)
        total = jnp.zeros(field.shape, jnp.float32)
        for offset in range(WIN):
            segment = field_halo[:, offset * LEAF : offset * LEAF + width].reshape(-1, leaves, LEAF)
            part_sum = jnp.einsum(
                "bij,rbj->rbi", tile_list[offset], segment, precision=lax.Precision.HIGHEST
            )
            total = total + part_sum.reshape(-1, width)
        return total

    def combine_levels(partials):
        count = len(partials)
        summed = []
        for index in range(count):
            total = partials[index]
            span_bits = index + 1
            for bit_pos in range(min(span_bits, col_bits)):
                total = total + partner(total, "col", bit_pos)
            for bit_pos in range(span_bits - col_bits):
                total = total + partner(total, "row", bit_pos)
            summed.append(total)
        return summed

    def far_field(field):
        total = jnp.zeros(field.shape, jnp.float32)
        partials = []
        for level in range(levels):
            cluster = LEAF * 2 ** (level + 1)
            if level + 1 - leaf_bits <= 0:
                grouped = basis[level].reshape(-1, width // cluster, cluster)
                values = field.reshape(-1, width // cluster, cluster)
                skeleton = jnp.einsum(
                    "kcs,rcs->crk", grouped, values, precision=lax.Precision.HIGHEST
                )
                spread_back = jnp.einsum(
                    "kcs,crk->rcs", grouped, skeleton, precision=lax.Precision.HIGHEST
                )
                total = total + spread_back.reshape(-1, width) / cluster
            else:
                partials.append(
                    jnp.einsum("kp,rp->rk", basis[level], field, precision=lax.Precision.HIGHEST)
                )
        summed = combine_levels(partials)
        for index in range(len(summed)):
            level = leaf_bits + index
            cluster = LEAF * 2 ** (level + 1)
            spread_back = jnp.einsum(
                "kp,rk->rp", basis[level], summed[index], precision=lax.Precision.HIGHEST
            )
            total = total + spread_back / cluster
        return total

    def operate(field):
        return nugget[None, :] * field + near_field(field) + far_field(field)

    def squares(values):
        return lax.psum(jnp.sum(values * values, axis=1), ("row", "col"))

    def iteration(step, carry):
        solution, residual, direction, norm_now = carry
        image = operate(direction)
        step_size = norm_now / lax.psum(jnp.sum(direction * image, axis=1), ("row", "col"))
        solution = solution + step_size[:, None] * direction
        residual = residual - step_size[:, None] * image
        norm_next = squares(residual)
        direction = residual + (norm_next / norm_now)[:, None] * direction
        return (solution, residual, direction, norm_next)

    start_state = (jnp.zeros(rhs.shape, jnp.float32), rhs, rhs, squares(rhs))
    solution, residual, direction, norm_now = lax.fori_loop(0, ITERS, iteration, start_state)
    return (solution, residual)


def solution(mesh):
    placed = (
        P(None, ("row", "col")),
        P(None, ("row", "col")),
        P(("row", "col")),
        P(("row", "col"), None),
        P(None, None, ("row", "col")),
    )
    return jax.shard_map(
        per_device,
        mesh=mesh,
        in_specs=placed,
        out_specs=(P(None, ("row", "col")), P(None, ("row", "col"))),
        check_vma=False,
    )
```

profile of v0, /device:TPU:1, one launch (start us, length us, event | category | flops | bytes accessed | tf_op | source)
XLA Modules:
  0.0 1176.0 jit_solution(4200081731278778201)
XLA Ops:
  9.8 80.7 %psum.29 = f32[32]{0:T(128)S(1)} all-reduce(f32[32]{0:T(128)S(1)} %multiply_reduce_fusion.5), channel_id=1, replica_groups=mesh['row'=32,'col'=8] {'row','col'}, use_global_device_ids=true, to_apply=%region_1.0 | all-reduce | flops 32 | bytes 256 | tf_op jit(solution)/shard_map/psum | solution.py:137
  91.3 11.3 copy.26
  102.6 1072.2 %while.21 = (s32[]{:T(128)}, f32[32,2048]{1,0:T(8,128)S(1)}, f32[32,2048]{1,0:T(8,128)S(1)}, f32[32,2048]{1,0:T(8,128)S(1)}, f32[32]{0:T(128)S(1)}, /*index=5*/f...) while((s32[]{:T(128)}, f32[32,2048]{1,0:T(8,128)S(1)}, ...), condition=%wide.wide.region_11.0_spmd.clone, body=%wide.wide.region_3.0_spmd.clone.sunk | while | flops 3264692224 | bytes 132829184 | solution.py:150
  126.6 9.5 multiply_reduce_fusion.12
  150.4 4.8 collective-permute-start.36
  171.0 7.7 fusion.326
  178.8 5.8 fusion.327
  184.6 5.6 fusion.328
  197.2 4.5 collective-permute-start.20
  218.8 78.8 %psum.36 = f32[32]{0:T(128)S(1)} all-reduce(f32[32]{0:T(128)S(1)} %get-tuple-element.406), channel_id=1, replica_groups=mesh['row'=32,'col'=8] {'row','col'}, use_global_device_ids=true, to_apply=%region_8.0 | all-reduce | flops 32 | bytes 256 | tf_op jit(solution)/shard_map/while/body/eval_jaxpr/psum | solution.py:142
  297.9 73.2 %psum.37 = f32[32]{0:T(128)S(1)} all-reduce(f32[32]{0:T(128)S(1)} %get-tuple-element.408), channel_id=1, replica_groups=mesh['row'=32,'col'=8] {'row','col'}, use_global_device_ids=true, to_apply=%region_10.0 | all-reduce | flops 32 | bytes 256 | tf_op jit(solution)/shard_map/while/body/eval_jaxpr/psum | solution.py:137
  394.8 9.5 multiply_reduce_fusion.12
  420.3 4.8 collective-permute-start.36
  439.2 7.7 fusion.326
  447.0 5.8 fusion.327
  452.8 5.7 fusion.328
  487.8 77.4 %psum.36 = f32[32]{0:T(128)S(1)} all-reduce(f32[32]{0:T(128)S(1)} %get-tuple-element.406), channel_id=1, replica_groups=mesh['row'=32,'col'=8] {'row','col'}, use_global_device_ids=true, to_apply=%region_8.0 | all-reduce | flops 32 | bytes 256 | tf_op jit(solution)/shard_map/while/body/eval_jaxpr/psum | solution.py:142
  565.4 73.2 %psum.37 = f32[32]{0:T(128)S(1)} all-reduce(f32[32]{0:T(128)S(1)} %get-tuple-element.408), channel_id=1, replica_groups=mesh['row'=32,'col'=8] {'row','col'}, use_global_device_ids=true, to_apply=%region_10.0 | all-reduce | flops 32 | bytes 256 | tf_op jit(solution)/shard_map/while/body/eval_jaxpr/psum | solution.py:137
  662.0 9.5 multiply_reduce_fusion.12
  688.2 4.8 collective-permute-start.36
  706.7 7.7 fusion.326
  714.5 5.8 fusion.327
  720.3 5.6 fusion.328
  755.3 77.1 %psum.36 = f32[32]{0:T(128)S(1)} all-reduce(f32[32]{0:T(128)S(1)} %get-tuple-element.406), channel_id=1, replica_groups=mesh['row'=32,'col'=8] {'row','col'}, use_global_device_ids=true, to_apply=%region_8.0 | all-reduce | flops 32 | bytes 256 | tf_op jit(solution)/shard_map/while/body/eval_jaxpr/psum | solution.py:142
  832.6 73.4 %psum.37 = f32[32]{0:T(128)S(1)} all-reduce(f32[32]{0:T(128)S(1)} %get-tuple-element.408), channel_id=1, replica_groups=mesh['row'=32,'col'=8] {'row','col'}, use_global_device_ids=true, to_apply=%region_10.0 | all-reduce | flops 32 | bytes 256 | tf_op jit(solution)/shard_map/while/body/eval_jaxpr/psum | solution.py:137
  929.6 9.5 multiply_reduce_fusion.12
  955.6 4.8 collective-permute-start.36
  974.4 7.7 fusion.326
  982.2 5.8 fusion.327
  988.0 5.6 fusion.328
  1022.8 77.1 %psum.36 = f32[32]{0:T(128)S(1)} all-reduce(f32[32]{0:T(128)S(1)} %get-tuple-element.406), channel_id=1, replica_groups=mesh['row'=32,'col'=8] {'row','col'}, use_global_device_ids=true, to_apply=%region_8.0 | all-reduce | flops 32 | bytes 256 | tf_op jit(solution)/shard_map/while/body/eval_jaxpr/psum | solution.py:142
  1100.2 73.4 %psum.37 = f32[32]{0:T(128)S(1)} all-reduce(f32[32]{0:T(128)S(1)} %get-tuple-element.408), channel_id=1, replica_groups=mesh['row'=32,'col'=8] {'row','col'}, use_global_device_ids=true, to_apply=%region_10.0 | all-reduce | flops 32 | bytes 256 | tf_op jit(solution)/shard_map/while/body/eval_jaxpr/psum | solution.py:137
  (616 shorter events, 336.3 us)
Async XLA Ops:
  2.3 100.3 %collective-permute-start.38 = (f32[3,512]{1,0:T(4,128)S(1)}, f32[3,512]{1,0:T(4,128)S(1)}, u32[]{:S(2)}, u32[]{:S(2)}) collective-permute-start(f32[3,512]{1,0:T(4,128)S(1)} %get-tuple-element.248), channel_id=1, source_target_pairs={{0,1},{1,2},{2,3},{3,4},{4,5},{5,6},{6,7},{7,8},{8,9},{9,10},{10,1... | collective-permute-start | bytes 18440 | tf_op jit(solution)/shard_map/ppermute | solution.py:24
  6.8 95.8 %collective-permute-start.39 = (f32[3,512]{1,0:T(4,128)S(1)}, f32[3,512]{1,0:T(4,128)S(1)}, u32[]{:S(2)}, u32[]{:S(2)}) collective-permute-start(f32[3,512]{1,0:T(4,128)S(1)} %get-tuple-element.249), channel_id=1, source_target_pairs={{1,0},{2,1},{3,2},{4,3},{5,4},{6,5},{7,6},{8,7},{9,8},{10,9},{11,1... | collective-permute-start | bytes 18440 | tf_op jit(solution)/shard_map/ppermute | solution.py:26
  105.0 33.0 %collective-permute-start.21 = (f32[32,128]{1,0:T(8,128)S(1)}, f32[32,128]{1,0:T(8,128)S(1)}, u32[]{:S(2)}, u32[]{:S(2)}) collective-permute-start(f32[32,128]{1,0:T(8,128)S(1)} %fusion.315), channel_id=1, source_target_pairs={{0,1},{1,0},{2,3},{3,2},{4,5},{5,4},{6,7},{7,6},{8,9},{9,8},{10,11... | collective-permute-start | bytes 49160 | tf_op jit(solution)/shard_map/while/body/eval_jaxpr/ppermute | solution.py:36
  108.1 30.0 %collective-permute-start.15 = (f32[32,128]{1,0:T(8,128)S(1)}, f32[32,128]{1,0:T(8,128)S(1)}, u32[]{:S(2)}, u32[]{:S(2)}) collective-permute-start(f32[32,128]{1,0:T(8,128)S(1)} %fusion.314), channel_id=1, source_target_pairs={{0,1},{1,0},{2,3},{3,2},{4,5},{5,4},{6,7},{7,6},{8,9},{9,8},{10,11... | collective-permute-start | bytes 49160 | tf_op jit(solution)/shard_map/while/body/eval_jaxpr/ppermute | solution.py:36
  110.1 28.5 %collective-permute-start.8 = (f32[32,128]{1,0:T(8,128)S(1)}, f32[32,128]{1,0:T(8,128)S(1)}, u32[]{:S(2)}, u32[]{:S(2)}) collective-permute-start(f32[32,128]{1,0:T(8,128)S(1)} %fusion.313), channel_id=1, source_target_pairs={{0,1},{1,0},{2,3},{3,2},{4,5},{5,4},{6,7},{7,6},{8,9},{9,8},{10,11... | collective-permute-start | bytes 49160 | tf_op jit(solution)/shard_map/while/body/eval_jaxpr/ppermute | solution.py:36
  112.6 27.9 %collective-permute-start.26 = (f32[32,128]{1,0:T(8,128)S(1)}, f32[32,128]{1,0:T(8,128)S(1)}, u32[]{:S(2)}, u32[]{:S(2)}) collective-permute-start(f32[32,128]{1,0:T(8,128)S(1)} %fusion.316), channel_id=1, source_target_pairs={{0,1},{1,0},{2,3},{3,2},{4,5},{5,4},{6,7},{7,6},{8,9},{9,8},{10,11... | collective-permute-start | bytes 49160 | tf_op jit(solution)/shard_map/while/body/eval_jaxpr/ppermute | solution.py:36
  168.2 25.1 %collective-permute-start.11 = (f32[32,128]{1,0:T(8,128)S(1)}, f32[32,128]{1,0:T(8,128)S(1)}, u32[]{:S(2)}, u32[]{:S(2)}) collective-permute-start(f32[32,128]{1,0:T(8,128)S(1)} %add.741), channel_id=1, source_target_pairs={{0,8},{8,0},{16,24},{24,16},{32,40},{40,32},{48,56},{56,48},{64,72... | collective-permute-start | bytes 49160 | tf_op jit(solution)/shard_map/while/body/eval_jaxpr/ppermute | solution.py:36
  169.0 26.8 %collective-permute-start.29 = (f32[32,128]{1,0:T(8,128)S(1)}, f32[32,128]{1,0:T(8,128)S(1)}, u32[]{:S(2)}, u32[]{:S(2)}) collective-permute-start(f32[32,128]{1,0:T(8,128)S(1)} %add.756), channel_id=1, source_target_pairs={{0,8},{8,0},{16,24},{24,16},{32,40},{40,32},{48,56},{56,48},{64,72... | collective-permute-start | bytes 49160 | tf_op jit(solution)/shard_map/while/body/eval_jaxpr/ppermute | solution.py:36
  190.2 27.3 %collective-permute-start.35 = (f32[32,128]{1,0:T(8,128)S(1)}, f32[32,128]{1,0:T(8,128)S(1)}, u32[]{:S(2)}, u32[]{:S(2)}) collective-permute-start(f32[32,128]{1,0:T(8,128)S(1)} %fusion.323), channel_id=1, source_target_pairs={{0,1},{1,0},{2,3},{3,2},{4,5},{5,4},{6,7},{7,6},{8,9},{9,8},{10,11... | collective-permute-start | bytes 49160 | tf_op jit(solution)/shard_map/while/body/eval_jaxpr/ppermute | solution.py:36
  373.4 32.8 %collective-permute-start.21 = (f32[32,128]{1,0:T(8,128)S(1)}, f32[32,128]{1,0:T(8,128)S(1)}, u32[]{:S(2)}, u32[]{:S(2)}) collective-permute-start(f32[32,128]{1,0:T(8,128)S(1)} %fusion.315), channel_id=1, source_target_pairs={{0,1},{1,0},{2,3},{3,2},{4,5},{5,4},{6,7},{7,6},{8,9},{9,8},{10,11... | collective-permute-start | bytes 49160 | tf_op jit(solution)/shard_map/while/body/eval_jaxpr/ppermute | solution.py:36
  376.0 30.3 %collective-permute-start.15 = (f32[32,128]{1,0:T(8,128)S(1)}, f32[32,128]{1,0:T(8,128)S(1)}, u32[]{:S(2)}, u32[]{:S(2)}) collective-permute-start(f32[32,128]{1,0:T(8,128)S(1)} %fusion.314), channel_id=1, source_target_pairs={{0,1},{1,0},{2,3},{3,2},{4,5},{5,4},{6,7},{7,6},{8,9},{9,8},{10,11... | collective-permute-start | bytes 49160 | tf_op jit(solution)/shard_map/while/body/eval_jaxpr/ppermute | solution.py:36
  378.0 28.8 %collective-permute-start.8 = (f32[32,128]{1,0:T(8,128)S(1)}, f32[32,128]{1,0:T(8,128)S(1)}, u32[]{:S(2)}, u32[]{:S(2)}) collective-permute-start(f32[32,128]{1,0:T(8,128)S(1)} %fusion.313), channel_id=1, source_target_pairs={{0,1},{1,0},{2,3},{3,2},{4,5},{5,4},{6,7},{7,6},{8,9},{9,8},{10,11... | collective-permute-start | bytes 49160 | tf_op jit(solution)/shard_map/while/body/eval_jaxpr/ppermute | solution.py:36
  380.5 28.5 %collective-permute-start.26 = (f32[32,128]{1,0:T(8,128)S(1)}, f32[32,128]{1,0:T(8,128)S(1)}, u32[]{:S(2)}, u32[]{:S(2)}) collective-permute-start(f32[32,128]{1,0:T(8,128)S(1)} %fusion.316), channel_id=1, source_target_pairs={{0,1},{1,0},{2,3},{3,2},{4,5},{5,4},{6,7},{7,6},{8,9},{9,8},{10,11... | collective-permute-start | bytes 49160 | tf_op jit(solution)/shard_map/while/body/eval_jaxpr/ppermute | solution.py:36
  382.5 24.9 %collective-permute-start.30 = (f32[32,128]{1,0:T(8,128)S(1)}, f32[32,128]{1,0:T(8,128)S(1)}, u32[]{:S(2)}, u32[]{:S(2)}) collective-permute-start(f32[32,128]{1,0:T(8,128)S(1)} %fusion.317), channel_id=1, source_target_pairs={{0,1},{1,0},{2,3},{3,2},{4,5},{5,4},{6,7},{7,6},{8,9},{9,8},{10,11... | collective-permute-start | bytes 49160 | tf_op jit(solution)/shard_map/while/body/eval_jaxpr/ppermute | solution.py:36
  437.4 26.1 %collective-permute-start.29 = (f32[32,128]{1,0:T(8,128)S(1)}, f32[32,128]{1,0:T(8,128)S(1)}, u32[]{:S(2)}, u32[]{:S(2)}) collective-permute-start(f32[32,128]{1,0:T(8,128)S(1)} %add.756), channel_id=1, source_target_pairs={{0,8},{8,0},{16,24},{24,16},{32,40},{40,32},{48,56},{56,48},{64,72... | collective-permute-start | bytes 49160 | tf_op jit(solution)/shard_map/while/body/eval_jaxpr/ppermute | solution.py:36
  458.5 28.0 %collective-permute-start.35 = (f32[32,128]{1,0:T(8,128)S(1)}, f32[32,128]{1,0:T(8,128)S(1)}, u32[]{:S(2)}, u32[]{:S(2)}) collective-permute-start(f32[32,128]{1,0:T(8,128)S(1)} %fusion.323), channel_id=1, source_target_pairs={{0,1},{1,0},{2,3},{3,2},{4,5},{5,4},{6,7},{7,6},{8,9},{9,8},{10,11... | collective-permute-start | bytes 49160 | tf_op jit(solution)/shard_map/while/body/eval_jaxpr/ppermute | solution.py:36
  640.9 32.6 %collective-permute-start.21 = (f32[32,128]{1,0:T(8,128)S(1)}, f32[32,128]{1,0:T(8,128)S(1)}, u32[]{:S(2)}, u32[]{:S(2)}) collective-permute-start(f32[32,128]{1,0:T(8,128)S(1)} %fusion.315), channel_id=1, source_target_pairs={{0,1},{1,0},{2,3},{3,2},{4,5},{5,4},{6,7},{7,6},{8,9},{9,8},{10,11... | collective-permute-start | bytes 49160 | tf_op jit(solution)/shard_map/while/body/eval_jaxpr/ppermute | solution.py:36
  643.5 30.0 %collective-permute-start.15 = (f32[32,128]{1,0:T(8,128)S(1)}, f32[32,128]{1,0:T(8,128)S(1)}, u32[]{:S(2)}, u32[]{:S(2)}) collective-permute-start(f32[32,128]{1,0:T(8,128)S(1)} %fusion.314), channel_id=1, source_target_pairs={{0,1},{1,0},{2,3},{3,2},{4,5},{5,4},{6,7},{7,6},{8,9},{9,8},{10,11... | collective-permute-start | bytes 49160 | tf_op jit(solution)/shard_map/while/body/eval_jaxpr/ppermute | solution.py:36
  645.5 28.6 %collective-permute-start.8 = (f32[32,128]{1,0:T(8,128)S(1)}, f32[32,128]{1,0:T(8,128)S(1)}, u32[]{:S(2)}, u32[]{:S(2)}) collective-permute-start(f32[32,128]{1,0:T(8,128)S(1)} %fusion.313), channel_id=1, source_target_pairs={{0,1},{1,0},{2,3},{3,2},{4,5},{5,4},{6,7},{7,6},{8,9},{9,8},{10,11... | collective-permute-start | bytes 49160 | tf_op jit(solution)/shard_map/while/body/eval_jaxpr/ppermute | solution.py:36
  648.0 28.6 %collective-permute-start.26 = (f32[32,128]{1,0:T(8,128)S(1)}, f32[32,128]{1,0:T(8,128)S(1)}, u32[]{:S(2)}, u32[]{:S(2)}) collective-permute-start(f32[32,128]{1,0:T(8,128)S(1)} %fusion.316), channel_id=1, source_target_pairs={{0,1},{1,0},{2,3},{3,2},{4,5},{5,4},{6,7},{7,6},{8,9},{9,8},{10,11... | collective-permute-start | bytes 49160 | tf_op jit(solution)/shard_map/while/body/eval_jaxpr/ppermute | solution.py:36
  650.0 25.0 %collective-permute-start.30 = (f32[32,128]{1,0:T(8,128)S(1)}, f32[32,128]{1,0:T(8,128)S(1)}, u32[]{:S(2)}, u32[]{:S(2)}) collective-permute-start(f32[32,128]{1,0:T(8,128)S(1)} %fusion.317), channel_id=1, source_target_pairs={{0,1},{1,0},{2,3},{3,2},{4,5},{5,4},{6,7},{7,6},{8,9},{9,8},{10,11... | collective-permute-start | bytes 49160 | tf_op jit(solution)/shard_map/while/body/eval_jaxpr/ppermute | solution.py:36
  703.9 24.8 %collective-permute-start.11 = (f32[32,128]{1,0:T(8,128)S(1)}, f32[32,128]{1,0:T(8,128)S(1)}, u32[]{:S(2)}, u32[]{:S(2)}) collective-permute-start(f32[32,128]{1,0:T(8,128)S(1)} %add.741), channel_id=1, source_target_pairs={{0,8},{8,0},{16,24},{24,16},{32,40},{40,32},{48,56},{56,48},{64,72... | collective-permute-start | bytes 49160 | tf_op jit(solution)/shard_map/while/body/eval_jaxpr/ppermute | solution.py:36
  705.0 26.3 %collective-permute-start.29 = (f32[32,128]{1,0:T(8,128)S(1)}, f32[32,128]{1,0:T(8,128)S(1)}, u32[]{:S(2)}, u32[]{:S(2)}) collective-permute-start(f32[32,128]{1,0:T(8,128)S(1)} %add.756), channel_id=1, source_target_pairs={{0,8},{8,0},{16,24},{24,16},{32,40},{40,32},{48,56},{56,48},{64,72... | collective-permute-start | bytes 49160 | tf_op jit(solution)/shard_map/while/body/eval_jaxpr/ppermute | solution.py:36
  725.9 28.0 %collective-permute-start.35 = (f32[32,128]{1,0:T(8,128)S(1)}, f32[32,128]{1,0:T(8,128)S(1)}, u32[]{:S(2)}, u32[]{:S(2)}) collective-permute-start(f32[32,128]{1,0:T(8,128)S(1)} %fusion.323), channel_id=1, source_target_pairs={{0,1},{1,0},{2,3},{3,2},{4,5},{5,4},{6,7},{7,6},{8,9},{9,8},{10,11... | collective-permute-start | bytes 49160 | tf_op jit(solution)/shard_map/while/body/eval_jaxpr/ppermute | solution.py:36
  908.5 32.5 %collective-permute-start.21 = (f32[32,128]{1,0:T(8,128)S(1)}, f32[32,128]{1,0:T(8,128)S(1)}, u32[]{:S(2)}, u32[]{:S(2)}) collective-permute-start(f32[32,128]{1,0:T(8,128)S(1)} %fusion.315), channel_id=1, source_target_pairs={{0,1},{1,0},{2,3},{3,2},{4,5},{5,4},{6,7},{7,6},{8,9},{9,8},{10,11... | collective-permute-start | bytes 49160 | tf_op jit(solution)/shard_map/while/body/eval_jaxpr/ppermute | solution.py:36
  911.2 30.0 %collective-permute-start.15 = (f32[32,128]{1,0:T(8,128)S(1)}, f32[32,128]{1,0:T(8,128)S(1)}, u32[]{:S(2)}, u32[]{:S(2)}) collective-permute-start(f32[32,128]{1,0:T(8,128)S(1)} %fusion.314), channel_id=1, source_target_pairs={{0,1},{1,0},{2,3},{3,2},{4,5},{5,4},{6,7},{7,6},{8,9},{9,8},{10,11... | collective-permute-start | bytes 49160 | tf_op jit(solution)/shard_map/while/body/eval_jaxpr/ppermute | solution.py:36
  913.1 28.5 %collective-permute-start.8 = (f32[32,128]{1,0:T(8,128)S(1)}, f32[32,128]{1,0:T(8,128)S(1)}, u32[]{:S(2)}, u32[]{:S(2)}) collective-permute-start(f32[32,128]{1,0:T(8,128)S(1)} %fusion.313), channel_id=1, source_target_pairs={{0,1},{1,0},{2,3},{3,2},{4,5},{5,4},{6,7},{7,6},{8,9},{9,8},{10,11... | collective-permute-start | bytes 49160 | tf_op jit(solution)/shard_map/while/body/eval_jaxpr/ppermute | solution.py:36
  915.6 28.6 %collective-permute-start.26 = (f32[32,128]{1,0:T(8,128)S(1)}, f32[32,128]{1,0:T(8,128)S(1)}, u32[]{:S(2)}, u32[]{:S(2)}) collective-permute-start(f32[32,128]{1,0:T(8,128)S(1)} %fusion.316), channel_id=1, source_target_pairs={{0,1},{1,0},{2,3},{3,2},{4,5},{5,4},{6,7},{7,6},{8,9},{9,8},{10,11... | collective-permute-start | bytes 49160 | tf_op jit(solution)/shard_map/while/body/eval_jaxpr/ppermute | solution.py:36
  917.6 24.9 %collective-permute-start.30 = (f32[32,128]{1,0:T(8,128)S(1)}, f32[32,128]{1,0:T(8,128)S(1)}, u32[]{:S(2)}, u32[]{:S(2)}) collective-permute-start(f32[32,128]{1,0:T(8,128)S(1)} %fusion.317), channel_id=1, source_target_pairs={{0,1},{1,0},{2,3},{3,2},{4,5},{5,4},{6,7},{7,6},{8,9},{9,8},{10,11... | collective-permute-start | bytes 49160 | tf_op jit(solution)/shard_map/while/body/eval_jaxpr/ppermute | solution.py:36
  971.3 25.0 %collective-permute-start.11 = (f32[32,128]{1,0:T(8,128)S(1)}, f32[32,128]{1,0:T(8,128)S(1)}, u32[]{:S(2)}, u32[]{:S(2)}) collective-permute-start(f32[32,128]{1,0:T(8,128)S(1)} %add.741), channel_id=1, source_target_pairs={{0,8},{8,0},{16,24},{24,16},{32,40},{40,32},{48,56},{56,48},{64,72... | collective-permute-start | bytes 49160 | tf_op jit(solution)/shard_map/while/body/eval_jaxpr/ppermute | solution.py:36
  972.4 26.4 %collective-permute-start.29 = (f32[32,128]{1,0:T(8,128)S(1)}, f32[32,128]{1,0:T(8,128)S(1)}, u32[]{:S(2)}, u32[]{:S(2)}) collective-permute-start(f32[32,128]{1,0:T(8,128)S(1)} %add.756), channel_id=1, source_target_pairs={{0,8},{8,0},{16,24},{24,16},{32,40},{40,32},{48,56},{56,48},{64,72... | collective-permute-start | bytes 49160 | tf_op jit(solution)/shard_map/while/body/eval_jaxpr/ppermute | solution.py:36
  993.6 27.9 %collective-permute-start.35 = (f32[32,128]{1,0:T(8,128)S(1)}, f32[32,128]{1,0:T(8,128)S(1)}, u32[]{:S(2)}, u32[]{:S(2)}) collective-permute-start(f32[32,128]{1,0:T(8,128)S(1)} %fusion.323), channel_id=1, source_target_pairs={{0,1},{1,0},{2,3},{3,2},{4,5},{5,4},{6,7},{7,6},{8,9},{9,8},{10,11... | collective-permute-start | bytes 49160 | tf_op jit(solution)/shard_map/while/body/eval_jaxpr/ppermute | solution.py:36
  (146 other events, 1804.0 us)
where the time goes:
time: 1180 us
  blocking collectives  684 us (58%)
  matrix products  207 us (18%)
  starting transfers between devices  199 us (17%)
  other arithmetic  40.7 us (3%)
  local copies, waits for them, and re-layouts  21.1 us (2%)
  waiting for transfers between devices  17.4 us (1%)
    psum x5, blocking collectives, squares(): return lax.psum(jnp.sum(values * values, axis=1), ('row', 'col'))  374 us
    psum x4, blocking collectives, iteration(): lax.psum(jnp.sum(direction * image, axis=1), ('row', 'col'))  310 us
    ppermute x144, starting transfers between devices, partner(): return lax.ppermute(value, axis, pairs)  166 us
    dot_general x12, matrix products, near_field(): jnp.einsum('bij,rbj->rbi', tile_list[offset], segment, precision=lax.Prec...  76.4 us
    dot_general x32, matrix products, far_field(): jnp.einsum('kp,rp->rk', basis[level], field, precision=lax.Precision.HIGH...  60 us
    dot_general x32, matrix products, far_field(): jnp.einsum('kp,rk->rp', basis[level], summed[index], precision=lax.Precis...  46.9 us
    reduce_sum x4, other arithmetic, tile_block(): square_dist = jnp.sum(spread * spread, axis=0)  38.2 us
  transfers between devices with their start and end apart: 154, of which 12 were waited for; matrix products, arithmetic and copies ran while one was open for 21% of the time, Pallas kernels for 0%

commit v1 on v0

v1 whole, which is shorter than its diff:
```python
import functools

import jax
import jax.numpy as jnp
from jax import lax
from jax.experimental import pallas as pl
from jax.experimental.pallas import tpu as pltpu
from jax.sharding import PartitionSpec as P

LEAF = 512
ITERS = 4
RANK = 128
NRHS = 32
LEVELS = 10
LEAVES = 4
WIDTH = LEAF * LEAVES
NC, NZ, NY = 8, 8, 4
NDEV = NC * NZ * NY
MESH = pl.DeviceIdType.MESH
F32 = jnp.float32
BF16 = jnp.bfloat16

ROOT_THREE = 1.7320508075688772
LENGTH = 1.6 * LEAF ** (-1.0 / 3.0)
LOG2E = 1.4426950408889634
STRIP = 32


def dot_nn(a, b):
    return lax.dot_general(a, b, (((1,), (0,)), ((), ())), preferred_element_type=F32)


def dot_nt(a, b):
    return lax.dot_general(a, b, (((1,), (1,)), ((), ())), preferred_element_type=F32)


def split3(value):
    first = value.astype(BF16)
    rest = value - first.astype(F32)
    second = rest.astype(BF16)
    third = (rest - second.astype(F32)).astype(BF16)
    return jnp.concatenate([first, second, third], axis=0)


def product(dot, pieces, high, low):
    rows = pieces.shape[0] // 3
    big = dot(pieces, high)
    small = dot(pieces[: 2 * rows], low)
    return (big[:rows] + (big[rows : 2 * rows] + small[:rows])) + (big[2 * rows :] + small[rows:])


def kernel(
    rhs_ref,
    coords_ref,
    nugget_ref,
    ids_ref,
    basis_ref,
    sol_ref,
    res_ref,
    stage,
    bh,
    bl,
    eh,
    el,
    ccol,
    chalo,
    fs,
    fh,
    dirn,
    wvec,
    qvec,
    zvec,
    halo,
    prs,
    p01,
    recv1,
    recv01,
    zsend,
    recv2,
    recv20,
    ysend,
    recv3,
    tfull,
    scs,
    scr,
    bsem,
    csem,
    hsem,
    s1,
    s01,
    s2,
    s20,
    s3,
    sg1,
    sg2,
    ssc,
    cs_send,
    hs_send,
    s1_send,
    s01_send,
    s2_send,
    s20_send,
    s3_send,
    sg1_send,
    sg2_send,
    ssc_send,
):
    row = lax.axis_index("row")
    col = lax.axis_index("col")
    yy = row // NZ
    zz = row % NZ
    hh = col // 4
    gg = col % 4
    dev = row * NC + col
    right_dev = (dev + 1) % NDEV
    left_dev = (dev + NDEV - 1) % NDEV
    right = (right_dev // NC, right_dev % NC)
    left = (left_dev // NC, left_dev % NC)
    cpeers = [(row, (col + k) % NC) for k in range(1, NC)]
    zpeers = [(yy * NZ + (zz + k) % NZ, col) for k in range(1, NZ)]
    ypeers = [(((yy + k) % NY) * NZ + zz, col) for k in range(1, NY)]
    quad = [(row, (col // 4) * 4 + (col % 4 + k) % 4) for k in range(1, 4)]
    core = (row, col + 1 - 2 * (col % 2))
    ztwin = (yy * NZ + zz + 1 - 2 * (zz % 2), col)
    my_rows = pl.ds(pl.multiple_of(gg * 8, 8), 8)

    order = list(range(2, LEVELS)) + [0, 1]
    for level in order:
        pltpu.make_async_copy(basis_ref.at[level], stage.at[level], bsem.at[level]).start()
    barrier = pltpu.get_barrier_semaphore()
    greeted = cpeers + zpeers + ypeers + [left, right]
    for peer in greeted:
        pl.semaphore_signal(barrier, inc=1, device_id=peer, device_id_type=MESH)

    def send(src, dst, send_sem, recv_sem, peer):
        pltpu.make_async_remote_copy(
            src_ref=src, dst_ref=dst, send_sem=send_sem, recv_sem=recv_sem, device_id=peer, device_id_type=MESH
        ).start()

    def await_bytes(ref, sem):
        pltpu.make_async_copy(ref, ref, sem).wait()

    lane = lax.broadcasted_iota(jnp.int32, (NRHS, 128), 1)
    sub = lax.broadcasted_iota(jnp.int32, (NRHS, 128), 0)
    hit = (lane % NRHS) == sub

    def as_row(columns):
        spread = jnp.zeros((NRHS, 128), F32)
        for index, column in enumerate(columns):
            spread = jnp.where(hit & (lane // NRHS == index), column, spread)
        return jnp.sum(spread, axis=0, keepdims=True)

    def as_columns(line):
        wide = jnp.where(hit, jnp.broadcast_to(line, (NRHS, 128)), 0.0)
        return [
            jnp.sum(jnp.where(lane // NRHS == index, wide, 0.0), axis=1, keepdims=True)
            for index in range(4)
        ]

    def dots_row():
        r, d, q = res_ref[...], dirn[...], qvec[...]
        return as_row(
            [
                jnp.sum(r * r, axis=1, keepdims=True),
                jnp.sum(d * q, axis=1, keepdims=True),
                jnp.sum(r * q, axis=1, keepdims=True),
                jnp.sum(q * q, axis=1, keepdims=True),
            ]
        )

    def scalar_send(a, phase, peers, base):
        for k, peer in enumerate(peers):
            send(scs.at[a, phase], scr.at[a, base + k], ssc_send.at[a, phase], ssc.at[a, phase], peer)

    def scalar_gather(a, phase, count, base):
        await_bytes(scr.at[a, pl.ds(base, count)], ssc.at[a, phase])
        total = scs[a, phase]
        for k in range(count):
            total = total + scr[a, base + k]
        return total

    def split_level(level):
        value = stage[level]
        rows = slice(level * RANK, (level + 1) * RANK)
        high = value.astype(BF16)
        bh[rows, :] = high
        bl[rows, :] = (value - high.astype(F32)).astype(BF16)

    def load_levels(levels):
        for level in levels:
            pltpu.make_async_copy(basis_ref.at[level], stage.at[level], bsem.at[level]).wait()
            split_level(level)

    def skeleton_pair(a, level):
        rows = slice(level * RANK, (level + 2) * RANK)
        both = product(dot_nt, fs[...], bh[rows, :], bl[rows, :])
        for side in range(2):
            part = both[:, side * RANK : (side + 1) * RANK]
            if level == 2:
                p01[a, side] = part
            else:
                prs[a, side, (level - 4) // 2] = part

    def spread(levels, total):
        scaled = jnp.concatenate([t * (1.0 / (LEAF * 2 ** (level + 1))) for level, t in zip(levels, total)], axis=1)
        pieces = split3(scaled)
        rows = slice(levels[0] * RANK, (levels[-1] + 1) * RANK)
        for start in range(0, WIDTH, 512):
            span = slice(start, start + 512)
            zvec[:, span] += product(dot_nn, pieces, bh[rows, span], bl[rows, span])

    def local_levels():
        for level, cluster in ((0, 2 * LEAF), (1, 4 * LEAF)):
            rows = slice(level * RANK, (level + 1) * RANK)
            for start in range(0, WIDTH, cluster):
                span = slice(start, start + cluster)
                skeleton = product(dot_nt, fs[:, span], bh[rows, span], bl[rows, span])
                pieces = split3(skeleton * (1.0 / cluster))
                zvec[:, span] += product(dot_nn, pieces, bh[rows, span], bl[rows, span])

    def mask_value(leaf, offset):
        target = dev * LEAVES + leaf + offset - 1
        found = (ids_ref[leaf, 0] == target) | (ids_ref[leaf, 1] == target) | (ids_ref[leaf, 2] == target)
        return jnp.where(found & (target >= 0), 1.0, 0.0).astype(F32)

    def near_term(leaf, offset, pieces, block, dot):
        span = slice(leaf * LEAF, (leaf + 1) * LEAF)
        zvec[:, span] += mask_value(leaf, offset) * product(dot, pieces, eh[block], el[block])

    def own_pieces(leaf):
        return fs[:, leaf * LEAF : (leaf + 1) * LEAF]

    def near_diag(leaf):
        near_term(leaf, 1, own_pieces(leaf), leaf, dot_nn)

    def near_pair(leaf):
        near_term(leaf + 1, 0, own_pieces(leaf), 5 + leaf, dot_nn)
        near_term(leaf, 2, own_pieces(leaf + 1), 5 + leaf, dot_nt)

    def near_halo(a):
        for side, leaf, offset, block in ((0, 0, 0, 4), (1, LEAVES - 1, 2, 8)):
            await_bytes(halo.at[a, side], hsem.at[a, side])
            fh[side] = split3(halo[a, side])
            near_term(leaf, offset, fh[side], block, dot_nt)

    def build(block, first_leaf, other):
        def strip(index, carry):
            start = pl.multiple_of(index * STRIP, STRIP)
            here = ccol[pl.ds(first_leaf * LEAF + start, STRIP), :]
            square = None
            for axis in range(3):
                gap = here[:, axis : axis + 1] - other(axis)
                square = gap * gap if square is None else square + gap * gap
            dist = square * lax.rsqrt(jnp.maximum(square, 1e-30))
            factor = ROOT_THREE / LENGTH
            value = (1.0 / 48.0 + (factor / 48.0) * dist) * jnp.exp2(dist * (-factor * LOG2E))
            high = value.astype(BF16)
            eh[block, pl.ds(start, STRIP), :] = high
            el[block, pl.ds(start, STRIP), :] = (value - high.astype(F32)).astype(BF16)
            return carry

        lax.fori_loop(0, LEAF // STRIP, strip, 0)

    def own_row(leaf):
        return lambda axis: coords_ref[axis : axis + 1, leaf * LEAF : (leaf + 1) * LEAF]

    def halo_row(side):
        return lambda axis: chalo[side, axis : axis + 1, :]

    def apply(a, first):
        fs[...] = split3(qvec[...])
        if first:
            for level in range(2, LEVELS, 2):
                load_levels([level, level + 1])
                skeleton_pair(a, level)
            pl.semaphore_wait(barrier, len(greeted))
        else:
            for level in range(2, LEVELS, 2):
                skeleton_pair(a, level)
        for k in range(1, NC):
            other = (col + k) % NC
            rows = pl.ds(pl.multiple_of((other % 4) * 8, 8), 8)
            send(prs.at[a, other // 4, :, rows, :], recv1.at[a, k - 1], s1_send.at[a], s1.at[a], cpeers[k - 1])
        if not first:
            scs[a, 0] = dots_row()
            scalar_send(a, 0, cpeers, 0)
        send(qvec.at[:, 0:LEAF], halo.at[a, 1], hs_send.at[a, 1], hsem.at[a, 1], left)
        send(qvec.at[:, WIDTH - LEAF : WIDTH], halo.at[a, 0], hs_send.at[a, 0], hsem.at[a, 0], right)
        send(p01.at[a, 0], recv01.at[a, 0], s01_send.at[a], s01.at[a], core)
        for k in range(3):
            send(p01.at[a, 1], recv01.at[a, k + 1], s01_send.at[a], s01.at[a], quad[k])
        if first:
            send(coords_ref.at[:, 0:LEAF], chalo.at[1], cs_send.at[1], csem.at[1], left)
            send(coords_ref.at[:, WIDTH - LEAF : WIDTH], chalo.at[0], cs_send.at[0], csem.at[0], right)

        zvec[...] = nugget_ref[...] * qvec[...]
        if first:
            ccol[...] = jnp.transpose(jnp.concatenate([coords_ref[...], jnp.zeros((5, WIDTH), F32)], axis=0))
            for leaf in range(LEAVES):
                build(leaf, leaf, own_row(leaf))
        for leaf in range(LEAVES):
            near_diag(leaf)

        await_bytes(recv1.at[a], s1.at[a])
        for t in range(3):
            total = prs[a, hh, t, my_rows, :]
            for k in range(NC - 1):
                total = total + recv1[a, k, t]
            zsend[a, t] = total
        for k in range(1, NZ):
            send(zsend.at[a, pl.ds(1, 2)], recv2.at[a, k - 1], s2_send.at[a], s2.at[a], zpeers[k - 1])
        send(zsend.at[a, 0], recv20.at[a], s20_send.at[a], s20.at[a], ztwin)
        if not first:
            scs[a, 1] = scalar_gather(a, 0, NC - 1, 0)
            scalar_send(a, 1, zpeers, NC - 1)

        if first:
            for leaf in range(LEAVES - 1):
                build(5 + leaf, leaf, own_row(leaf + 1))
        for leaf in range(LEAVES - 1):
            near_pair(leaf)

        await_bytes(recv2.at[a], s2.at[a])
        await_bytes(recv20.at[a], s20.at[a])
        one = zsend[a, 1]
        two = zsend[a, 2]
        for k in range(1, NZ):
            source = (zz + NZ - k) % NZ
            near_z = jnp.where((hh == 1) | (source // 4 == zz // 4), 1.0, 0.0).astype(F32)
            one = one + near_z * recv2[a, k - 1, 0]
            two = two + recv2[a, k - 1, 1]
        ysend[a] = two
        for k in range(1, NY):
            send(ysend.at[a], recv3.at[a, k - 1], s3_send.at[a], s3.at[a], ypeers[k - 1])
        tfull[a, hh, 0, my_rows, :] = zsend[a, 0] + hh.astype(F32) * recv20[a]
        tfull[a, hh, 1, my_rows, :] = one
        mine = tfull.at[a, hh, pl.ds(0, 2), my_rows, :]
        for k in range(1, NC):
            send(mine, mine, sg1_send.at[a], sg1.at[a], cpeers[k - 1])
        if not first:
            scs[a, 2] = scalar_gather(a, 1, NZ - 1, NC - 1)
            scalar_send(a, 2, ypeers, NC + NZ - 2)

        if first:
            load_levels([0, 1])
            for side, leaf, block in ((0, 0, 4), (1, LEAVES - 1, 8)):
                await_bytes(chalo.at[side], csem.at[side])
                build(block, leaf, halo_row(side))
        local_levels()

        await_bytes(recv3.at[a], s3.at[a])
        top = ysend[a]
        for k in range(1, NY):
            source = (yy + NY - k) % NY
            near_y = jnp.where((hh == 1) | (source // 2 == yy // 2), 1.0, 0.0).astype(F32)
            top = top + near_y * recv3[a, k - 1]
        tfull[a, hh, 2, my_rows, :] = top
        mine = tfull.at[a, hh, 2, my_rows, :]
        for k in range(1, NC):
            send(mine, mine, sg2_send.at[a], sg2.at[a], cpeers[k - 1])

        near_halo(a)
        await_bytes(recv01.at[a], s01.at[a])
        await_bytes(recv1.at[a, :, pl.ds(0, 2)], sg1.at[a])
        lower = [
            p01[a, 0] + recv01[a, 0],
            (p01[a, 1] + recv01[a, 1]) + (recv01[a, 2] + recv01[a, 3]),
            tfull[a, 0, 0],
            tfull[a, 1, 0],
            tfull[a, 0, 1],
            tfull[a, 1, 1],
        ]
        spread(list(range(2, 8)), lower)
        await_bytes(recv1.at[a, :, 0], sg2.at[a])
        spread([8, 9], [tfull[a, 0, 2], tfull[a, 1, 2]])

    def steps(total):
        norm, curve, cross, square = as_columns(total)
        step = norm / curve
        fresh = jnp.maximum(norm - 2.0 * step * cross + step * step * square, 0.0)
        return step, fresh / norm

    start = rhs_ref[...]
    sol_ref[...] = jnp.zeros_like(sol_ref)
    res_ref[...] = start
    dirn[...] = start
    qvec[...] = start
    apply(0, True)
    image = zvec[...]
    await_bytes(halo.at[0, 0], hs_send.at[0, 0])
    await_bytes(halo.at[0, 1], hs_send.at[0, 1])
    wvec[...] = image
    qvec[...] = image

    def iteration(a, carry):
        apply(a, False)
        total = scalar_gather(a, 2, NY - 1, NC + NZ - 2)
        step, ratio = steps(total)
        await_bytes(halo.at[a, 0], hs_send.at[a, 0])
        await_bytes(halo.at[a, 1], hs_send.at[a, 1])
        q = qvec[...]
        d = dirn[...]
        sol_ref[...] += step * d
        r = res_ref[...] - step * q
        res_ref[...] = r
        dirn[...] = r + ratio * d
        w = wvec[...] - step * zvec[...]
        wvec[...] = w
        qvec[...] = w + ratio * q
        return carry

    lax.fori_loop(1, ITERS, iteration, 0)

    last = ITERS
    scs[last, 0] = dots_row()
    scalar_send(last, 0, cpeers, 0)
    scs[last, 1] = scalar_gather(last, 0, NC - 1, 0)
    scalar_send(last, 1, zpeers, NC - 1)
    scs[last, 2] = scalar_gather(last, 1, NZ - 1, NC - 1)
    scalar_send(last, 2, ypeers, NC + NZ - 2)
    step, _ = steps(scalar_gather(last, 2, NY - 1, NC + NZ - 2))
    sol_ref[...] += step * dirn[...]
    res_ref[...] += -step * qvec[...]

    def drain(a, carry):
        await_bytes(recv1.at[a], s1_send.at[a])
        await_bytes(recv01.at[a], s01_send.at[a])
        await_bytes(recv2.at[a], s2_send.at[a])
        await_bytes(recv20.at[a], s20_send.at[a])
        await_bytes(recv3.at[a], s3_send.at[a])
        await_bytes(recv1.at[a, :, pl.ds(0, 2)], sg1_send.at[a])
        await_bytes(recv1.at[a, :, 0], sg2_send.at[a])
        return carry

    def drain_scalars(a, carry):
        for phase, (base, count) in enumerate(((0, NC - 1), (NC - 1, NZ - 1), (NC + NZ - 2, NY - 1))):
            await_bytes(scr.at[a, pl.ds(base, count)], ssc_send.at[a, phase])
        return carry

    lax.fori_loop(0, ITERS, drain, 0)
    lax.fori_loop(1, ITERS + 1, drain_scalars, 0)
    for side in range(2):
        await_bytes(chalo.at[side], cs_send.at[side])


def per_device(rhs, coords, nugget, near_ids, basis):
    vmem = pl.BlockSpec(memory_space=pltpu.VMEM)
    state = pltpu.VMEM((NRHS, WIDTH), F32)
    dma = pltpu.SemaphoreType.DMA
    n = ITERS
    scratch = [
        pltpu.VMEM((LEVELS, RANK, WIDTH), F32),
        pltpu.VMEM((LEVELS * RANK, WIDTH), BF16),
        pltpu.VMEM((LEVELS * RANK, WIDTH), BF16),
        pltpu.VMEM((9, LEAF, LEAF), BF16),
        pltpu.VMEM((9, LEAF, LEAF), BF16),
        pltpu.VMEM((WIDTH, 8), F32),
        pltpu.VMEM((2, 3, LEAF), F32),
        pltpu.VMEM((3 * NRHS, WIDTH), BF16),
        pltpu.VMEM((2, 3 * NRHS, LEAF), BF16),
        state,
        state,
        state,
        state,
        pltpu.VMEM((n, 2, NRHS, LEAF), F32),
        pltpu.VMEM((n, 2, 3, NRHS, RANK), F32),
        pltpu.VMEM((n, 2, NRHS, RANK), F32),
        pltpu.VMEM((n, NC - 1, 3, 8, RANK), F32),
        pltpu.VMEM((n, 4, NRHS, RANK), F32),
        pltpu.VMEM((n, 3, 8, RANK), F32),
        pltpu.VMEM((n, NZ - 1, 2, 8, RANK), F32),
        pltpu.VMEM((n, 8, RANK), F32),
        pltpu.VMEM((n, 8, RANK), F32),
        pltpu.VMEM((n, NY - 1, 8, RANK), F32),
        pltpu.VMEM((n, 2, 3, NRHS, RANK), F32),
        pltpu.VMEM((n + 1, 3, 1, RANK), F32),
        pltpu.VMEM((n + 1, NC + NZ + NY - 3, 1, RANK), F32),
        dma((LEVELS,)),
        dma((2,)),
        dma((n, 2)),
        dma((n,)),
        dma((n,)),
        dma((n,)),
        dma((n,)),
        dma((n,)),
        dma((n,)),
        dma((n,)),
        dma((n + 1, 3)),
        dma((2,)),
        dma((n, 2)),
        dma((n,)),
        dma((n,)),
        dma((n,)),
        dma((n,)),
        dma((n,)),
        dma((n,)),
        dma((n,)),
        dma((n + 1, 3)),
    ]
    return pl.pallas_call(
        kernel,
        out_shape=[jax.ShapeDtypeStruct((NRHS, WIDTH), F32)] * 2,
        in_specs=[
            vmem,
            vmem,
            vmem,
            pl.BlockSpec(memory_space=pltpu.SMEM),
            pl.BlockSpec(memory_space=pl.ANY),
        ],
        out_specs=[vmem, vmem],
        scratch_shapes=scratch,
        compiler_params=pltpu.CompilerParams(
            collective_id=0, has_side_effects=True, vmem_limit_bytes=56 * 1024 * 1024
        ),
    )(rhs, coords, nugget.reshape(1, WIDTH), near_ids, basis)


def solution(mesh):
    placed = (
        P(None, ("row", "col")),
        P(None, ("row", "col")),
        P(("row", "col")),
        P(("row", "col"), None),
        P(None, None, ("row", "col")),
    )
    return jax.shard_map(
        per_device,
        mesh=mesh,
        in_specs=placed,
        out_specs=(P(None, ("row", "col")), P(None, ("row", "col"))),
        check_vma=False,
    )
```

time: 1180 us -> 115 us (0.10)
  blocking collectives: 684 us -> 0 us
  matrix products: 207 us -> 0 us
  starting transfers between devices: 199 us -> 0 us
  Pallas kernels: 0 us -> 110 us
  other arithmetic: 40.7 us -> 0 us
  local copies, waits for them, and re-layouts: 21.1 us -> 3.34 us
  waiting for transfers between devices: 17.4 us -> 0 us
    psum x9 -> x0, blocking collectives: 684 us -> none  [the longest x5 374 us: squares(): return lax.psum(jnp.sum(values * values, axis=1), ('row', 'col'))]
    dot_general x92 -> x0, matrix products: 207 us -> none  [the longest x12 76.4 us: near_field(): jnp.einsum('bij,rbj->rbi', tile_list[offset], segment, precision=lax.Prec...]
    ppermute x154 -> x0, starting transfers between devices: 199 us -> none  [the longest x144 166 us: partner(): return lax.ppermute(value, axis, pairs)]
    pallas_call x0 -> x1, Pallas kernels: none -> 110 us  [per_device(): pl.pallas_call(kernel, out_shape=[jax.ShapeDtypeStruct((NRHS, WIDTH), F32...]
    reduce_sum x9 -> x0, other arithmetic: 39.3 us -> none  [the longest x4 38.2 us: tile_block(): square_dist = jnp.sum(spread * spread, axis=0)]
    ppermute x154 -> x0, waiting for transfers between devices: 17.4 us -> none  [the longest x144 17.4 us: partner(): return lax.ppermute(value, axis, pairs)]
  transfers between devices with their start and end apart: 154 -> 0, of which waited for: 12 -> 0; matrix products, arithmetic and copies ran while one was open for 21% -> 0% of each run, Pallas kernels for 0% -> 0%
where the time goes in v1:
time: 115 us; the launch traced here: 114 us
  Pallas kernels  110 us (96%)
  local copies, waits for them, and re-layouts  3.34 us (3%)
    pallas_call x1, Pallas kernels, per_device(): pl.pallas_call(kernel, out_shape=[jax.ShapeDtypeStruct((NRHS, WIDTH), F32...  110 us
    unnamed x2, local copies, waits for them, and re-layouts  3.34 us

profile of v1, /device:TPU:1, one launch (start us, length us, event | category | flops | bytes accessed | tf_op | source)
XLA Modules:
  0.0 114.4 jit_solution(10980856264388587397)
XLA Ops:
  0.6 110.4 %shard_map.68 = (f32[32,2048]{1,0:T(8,128)}, f32[32,2048]{1,0:T(8,128)}) custom-call(f32[32,2048]{1,0:T(8,128)} %rhs_ref.1, f32[3,2048]{1,0:T(4,128)} %coords_ref.1, f32[1,2048]{1,0:T(1,128)} %bitcast.1, s32[4,3]{1,0:T(4,128)} %ids_ref.1, f32[10,128,2048]{2,1,0:T(8,128)} %basis_ref.1), custom_call_target="tpu_custom_call" | custom-call | tf_op jit(solution)/shard_map/pallas_call | solution.py:500
  111.0 1.7 %copy.9 = f32[32,2048]{1,0:T(8,128)} copy(f32[32,2048]{1,0:T(8,128)} %get-tuple-element.4) | data formatting | bytes 524288
  112.7 1.7 %copy.10 = f32[32,2048]{1,0:T(8,128)} copy(f32[32,2048]{1,0:T(8,128)} %get-tuple-element.5) | data formatting | bytes 524288

commit v2 on v1

v2 whole, which is shorter than its diff:
```python
import functools

import jax
import jax.numpy as jnp
from jax import lax
from jax.experimental import pallas as pl
from jax.experimental.pallas import tpu as pltpu
from jax.sharding import PartitionSpec as P

LEAF = 512
ITERS = 4
RANK = 128
NRHS = 32
LEVELS = 10
LEAVES = 4
WIDTH = LEAF * LEAVES
NC, NZ, NY = 8, 8, 4
NDEV = NC * NZ * NY
MESH = pl.DeviceIdType.MESH
F32 = jnp.float32
BF16 = jnp.bfloat16

ROOT_THREE = 1.7320508075688772
LENGTH = 1.6 * LEAF ** (-1.0 / 3.0)
LOG2E = 1.4426950408889634
SCALE = ROOT_THREE / LENGTH * LOG2E


def dot_nn(a, b):
    return lax.dot_general(a, b, (((1,), (0,)), ((), ())), preferred_element_type=F32)


def dot_nt(a, b):
    return lax.dot_general(a, b, (((1,), (1,)), ((), ())), preferred_element_type=F32)


def thirds(value):
    first = value.astype(BF16)
    rest = value - first.astype(F32)
    second = rest.astype(BF16)
    third = (rest - second.astype(F32)).astype(BF16)
    return first, second, third


def split3(value):
    return jnp.concatenate(thirds(value), axis=0)


def product(dot, pieces, high, low):
    rows = pieces.shape[0] // 3
    big = dot(pieces, high)
    small = dot(pieces[: 2 * rows], low)
    return (big[:rows] + (big[rows : 2 * rows] + small[:rows])) + (big[2 * rows :] + small[rows:])


def ring(distance, count):
    return min(distance, count - distance)


FAR = sorted(
    [(j, k) for j in range(NY) for k in range(NZ) if j + k > 0],
    key=lambda jk: (-ring(jk[0], NY) - ring(jk[1], NZ), jk),
)
LINES = (NC - 1) + len(FAR)


def kernel(
    rhs_hbm,
    coords_hbm,
    nugget_hbm,
    ids_ref,
    basis_ref,
    sol_ref,
    res_ref,
    stage,
    bh,
    bl,
    th,
    tl,
    cext,
    nugget_ref,
    chalo,
    fs,
    dirn,
    wvec,
    qvec,
    zvec,
    halo,
    prs,
    p01,
    recv_top,
    recv_low,
    recv01,
    twin_send,
    recv_twin,
    recv_z,
    ysend,
    recv_y,
    tfull,
    scs,
    scr,
    bsem,
    isem,
    csem,
    hsem,
    s_top,
    s_low,
    s01,
    s_twin,
    s_z,
    s_y,
    sg1,
    sg2,
    ssc,
    cs_send,
    hs_send,
    s_top_send,
    s_low_send,
    s01_send,
    s_twin_send,
    s_z_send,
    s_y_send,
    sg1_send,
    sg2_send,
    ssc_send,
):
    row = lax.axis_index("row")
    col = lax.axis_index("col")
    yy = row // NZ
    zz = row % NZ
    hh = col // 4
    gg = col % 4
    dev = row * NC + col
    right_dev = (dev + 1) % NDEV
    left_dev = (dev + NDEV - 1) % NDEV
    right = (right_dev // NC, right_dev % NC)
    left = (left_dev // NC, left_dev % NC)
    cpeers = [(row, (col + k) % NC) for k in range(1, NC)]
    zpeers = [(yy * NZ + (zz + k) % NZ, col) for k in range(1, NZ)]
    ypeers = [(((yy + k) % NY) * NZ + zz, col) for k in range(1, NY)]
    fpeers = [(((yy + j) % NY) * NZ + (zz + k) % NZ, col) for j, k in FAR]
    quad = [(row, (col // 4) * 4 + (col % 4 + k) % 4) for k in range(1, 4)]
    core = (row, col + 1 - 2 * (col % 2))
    twin = (yy * NZ + zz + 1 - 2 * (zz % 2), col)
    my_rows = pl.ds(pl.multiple_of(gg * 8, 8), 8)

    loads = [
        pltpu.make_async_copy(rhs_hbm, qvec, isem.at[0]),
        pltpu.make_async_copy(coords_hbm, cext.at[:, LEAF : LEAF + WIDTH], isem.at[1]),
        pltpu.make_async_copy(nugget_hbm, nugget_ref, isem.at[2]),
    ]
    loads[0].start()
    for level in (8, 9, 6, 7, 4, 5, 2, 3, 0, 1):
        pltpu.make_async_copy(basis_ref.at[level], stage.at[level], bsem.at[level]).start()
    loads[1].start()
    loads[2].start()
    barrier = pltpu.get_barrier_semaphore()
    greeted = fpeers + cpeers + [left, right]
    for peer in greeted:
        pl.semaphore_signal(barrier, inc=1, device_id=peer, device_id_type=MESH)

    def send(src, dst, send_sem, recv_sem, peer):
        pltpu.make_async_remote_copy(
            src_ref=src, dst_ref=dst, send_sem=send_sem, recv_sem=recv_sem, device_id=peer, device_id_type=MESH
        ).start()

    def await_bytes(ref, sem):
        pltpu.make_async_copy(ref, ref, sem).wait()

    lane = lax.broadcasted_iota(jnp.int32, (NRHS, 128), 1)
    sub = lax.broadcasted_iota(jnp.int32, (NRHS, 128), 0)
    hit = (lane % NRHS) == sub

    def as_row(columns):
        spread = jnp.zeros((NRHS, 128), F32)
        for index, column in enumerate(columns):
            spread = jnp.where(hit & (lane // NRHS == index), column, spread)
        return jnp.sum(spread, axis=0, keepdims=True)

    def as_columns(line):
        wide = jnp.where(hit, jnp.broadcast_to(line, (NRHS, 128)), 0.0)
        return [
            jnp.sum(jnp.where(lane // NRHS == index, wide, 0.0), axis=1, keepdims=True)
            for index in range(4)
        ]

    def dots_row():
        r, d, q = res_ref[...], dirn[...], qvec[...]
        return as_row(
            [
                jnp.sum(r * r, axis=1, keepdims=True),
                jnp.sum(d * q, axis=1, keepdims=True),
                jnp.sum(r * q, axis=1, keepdims=True),
                jnp.sum(q * q, axis=1, keepdims=True),
            ]
        )

    def scalar_send(a, phase, peers, base):
        for k, peer in enumerate(peers):
            send(scs.at[a, phase], scr.at[a, base + k], ssc_send.at[a, phase], ssc.at[a, phase], peer)

    def scalar_gather(a, phase, count, base):
        await_bytes(scr.at[a, pl.ds(base, count)], ssc.at[a, phase])
        total = scs[a, phase]
        for k in range(count):
            total = total + scr[a, base + k]
        return total

    def load_levels(levels):
        for level in levels:
            pltpu.make_async_copy(basis_ref.at[level], stage.at[level], bsem.at[level]).wait()
            value = stage[level]
            rows = slice(level * RANK, (level + 1) * RANK)
            high = value.astype(BF16)
            bh[rows, :] = high
            bl[rows, :] = (value - high.astype(F32)).astype(BF16)

    def own(start, width):
        return fs[:, LEAF + start : LEAF + start + width]

    def skeleton_pair(a, level):
        rows = slice(level * RANK, (level + 2) * RANK)
        both = product(dot_nt, own(0, WIDTH), bh[rows, :], bl[rows, :])
        for side in range(2):
            part = both[:, side * RANK : (side + 1) * RANK]
            if level == 2:
                p01[a, side] = part
            else:
                prs[a, side, (level - 4) // 2] = part

    def scaled_pieces(levels, total):
        scaled = jnp.concatenate([t * (1.0 / (LEAF * 2 ** (level + 1))) for level, t in zip(levels, total)], axis=1)
        return split3(scaled), slice(levels[0] * RANK, (levels[-1] + 1) * RANK)

    def spread(levels, total):
        pieces, rows = scaled_pieces(levels, total)
        for start in range(0, WIDTH, 512):
            span = slice(start, start + 512)
            zvec[:, span] += product(dot_nn, pieces, bh[rows, span], bl[rows, span])

    def local_levels():
        for level, cluster in ((0, 2 * LEAF), (1, 4 * LEAF)):
            rows = slice(level * RANK, (level + 1) * RANK)
            for start in range(0, WIDTH, cluster):
                span = slice(start, start + cluster)
                skeleton = product(dot_nt, own(start, cluster), bh[rows, span], bl[rows, span])
                pieces = split3(skeleton * (1.0 / cluster))
                zvec[:, span] += product(dot_nn, pieces, bh[rows, span], bl[rows, span])

    def mask_value(leaf, offset):
        target = dev * LEAVES + leaf + offset - 1
        found = (ids_ref[leaf, 0] == target) | (ids_ref[leaf, 1] == target) | (ids_ref[leaf, 2] == target)
        return jnp.where(found & (target >= 0), 1.0, 0.0).astype(F32)

    def near(leaf):
        span = slice(leaf * LEAF, (leaf + 1) * LEAF)
        window = fs[:, leaf * LEAF : (leaf + 3) * LEAF]
        zvec[:, span] += product(dot_nn, window, th[leaf], tl[leaf])

    def take_halo(a, side):
        await_bytes(halo.at[a, side], hsem.at[a, side])
        start = side * (LEAF + WIDTH)
        fs[:, start : start + LEAF] = split3(halo[a, side])

    def center(leaf):
        first = cext[:, LEAF * (leaf + 1) : LEAF * (leaf + 1) + 128]
        return jnp.floor(first[:, 0:1]) + 0.5

    def features(points):
        parts = [part.astype(F32) for part in thirds(points)]
        norm = jnp.sum(points * points, axis=0, keepdims=True)
        return parts, [part.astype(F32) for part in thirds(norm)]

    def build(leaf):
        middle = center(leaf)
        (one, two, three), norms = features((cext[:, LEAF * (leaf + 1) : LEAF * (leaf + 2)] - middle) * SCALE)
        ones = jnp.ones((3, LEAF), F32)
        blank = jnp.zeros((8, LEAF), F32)
        here = jnp.concatenate([one, two, one, two, three, one], axis=0) * -2.0
        here = jnp.concatenate([here, ones] + norms + [blank], axis=0).astype(BF16)

        def block(offset, carry):
            start = pl.multiple_of((leaf + offset) * LEAF, LEAF)
            (one, two, three), norms = features((cext[:, pl.ds(start, LEAF)] - middle) * SCALE)
            there = jnp.concatenate([one, one, two, two, one, three] + norms + [ones, blank], axis=0)
            square = dot_nn(jnp.transpose(there).astype(BF16), here)
            square = jnp.maximum(square, 1e-30)
            dist = square * lax.rsqrt(square)
            weight = mask_value(leaf, offset) * (1.0 / 48.0)
            value = (weight + (weight * (1.0 / LOG2E)) * dist) * jnp.exp2(-dist)
            high = value.astype(BF16)
            rows = pl.ds(pl.multiple_of(offset * LEAF, LEAF), LEAF)
            th[leaf, rows, :] = high
            tl[leaf, rows, :] = (value - high.astype(F32)).astype(BF16)
            return carry

        lax.fori_loop(0, 3, block, 0)

    def eighth(k):
        other = (col + k) % NC
        return other // 4, pl.ds(pl.multiple_of((other % 4) * 8, 8), 8)

    def apply(a, first):
        if first:
            for level in (8, 6, 4, 2):
                load_levels([level, level + 1])
                skeleton_pair(a, level)
            pl.semaphore_wait(barrier, len(greeted))
        else:
            skeleton_pair(a, 8)
            skeleton_pair(a, 6)
        for k in range(1, NC):
            half, rows = eighth(k)
            part = prs.at[a, half, pl.ds(1, 2), rows, :]
            send(part, recv_top.at[a, k - 1], s_top_send.at[a], s_top.at[a], cpeers[k - 1])
        if not first:
            scs[a, 0] = dots_row()
            scalar_send(a, 0, cpeers, 0)
            skeleton_pair(a, 4)
        for k in range(1, NC):
            half, rows = eighth(k)
            send(prs.at[a, half, 0, rows, :], recv_low.at[a, k - 1], s_low_send.at[a], s_low.at[a], cpeers[k - 1])
        send(qvec.at[:, 0:LEAF], halo.at[a, 1], hs_send.at[a, 1], hsem.at[a, 1], left)
        send(qvec.at[:, WIDTH - LEAF : WIDTH], halo.at[a, 0], hs_send.at[a, 0], hsem.at[a, 0], right)
        if first:
            loads[1].wait()
            loads[2].wait()
            send(cext.at[:, LEAF : 2 * LEAF], chalo.at[1], cs_send.at[1], csem.at[1], left)
            send(cext.at[:, WIDTH : WIDTH + LEAF], chalo.at[0], cs_send.at[0], csem.at[0], right)
        else:
            skeleton_pair(a, 2)
        send(p01.at[a, 0], recv01.at[a, 0], s01_send.at[a], s01.at[a], core)
        for k in range(3):
            send(p01.at[a, 1], recv01.at[a, k + 1], s01_send.at[a], s01.at[a], quad[k])

        def edge(side):
            leaf = side * (LEAVES - 1)
            if first:
                await_bytes(chalo.at[side], csem.at[side])
                start = side * (LEAF + WIDTH)
                cext[:, start : start + LEAF] = chalo[side]
                build(leaf)
            take_halo(a, side)
            near(leaf)

        zvec[...] = nugget_ref[...] * qvec[...]
        if first:
            build(1)
        near(1)

        await_bytes(recv_top.at[a], s_top.at[a])
        for t in range(2):
            total = prs[a, hh, t + 1, my_rows, :]
            for k in range(NC - 1):
                total = total + recv_top[a, k, t]
            ysend[a, t] = total
        for n, (j, k) in enumerate(FAR):
            if j == 0:
                send(ysend.at[a], recv_z.at[a, k - 1], s_z_send.at[a], s_z.at[a], fpeers[n])
            else:
                slot = (j - 1) * NZ + k
                send(ysend.at[a, 1], recv_y.at[a, slot], s_y_send.at[a], s_y.at[a], fpeers[n])
        if not first:
            scs[a, 1] = scalar_gather(a, 0, NC - 1, 0)
            scalar_send(a, 1, zpeers, NC - 1)
        await_bytes(recv_low.at[a], s_low.at[a])
        total = prs[a, hh, 0, my_rows, :]
        for k in range(NC - 1):
            total = total + recv_low[a, k]
        twin_send[a] = total
        send(twin_send.at[a], recv_twin.at[a], s_twin_send.at[a], s_twin.at[a], twin)

        if first:
            build(2)
        near(2)
        edge(0)
        if not first:
            edge(1)
        await_bytes(recv_twin.at[a], s_twin.at[a])
        tfull[a, hh, 0, my_rows, :] = twin_send[a] + hh.astype(F32) * recv_twin[a]
        mine = tfull.at[a, hh, 0, my_rows, :]
        for k in range(1, NC):
            send(mine, mine, sg1_send.at[a], sg1.at[a], cpeers[k - 1])
        if first:
            load_levels([0, 1])
        local_levels()
        if not first:
            scs[a, 2] = scalar_gather(a, 1, NZ - 1, NC - 1)
            scalar_send(a, 2, ypeers, NC + NZ - 2)

        await_bytes(recv_z.at[a], s_z.at[a])
        await_bytes(recv_y.at[a], s_y.at[a])
        one = ysend[a, 0]
        two = ysend[a, 1]
        for k in range(1, NZ):
            source = (zz + NZ - k) % NZ
            quarter = jnp.where((hh == 1) | (source // 4 == zz // 4), 1.0, 0.0).astype(F32)
            one = one + quarter * recv_z[a, k - 1, 0]
            two = two + recv_z[a, k - 1, 1]
        for j in range(1, NY):
            source = (yy + NY - j) % NY
            half = jnp.where((hh == 1) | (source // 2 == yy // 2), 1.0, 0.0).astype(F32)
            ring_sum = recv_y[a, (j - 1) * NZ]
            for k in range(1, NZ):
                ring_sum = ring_sum + recv_y[a, (j - 1) * NZ + k]
            two = two + half * ring_sum
        tfull[a, hh, 1, my_rows, :] = one
        tfull[a, hh, 2, my_rows, :] = two
        mine = tfull.at[a, hh, pl.ds(1, 2), my_rows, :]
        for k in range(1, NC):
            send(mine, mine, sg2_send.at[a], sg2.at[a], cpeers[k - 1])

        if first:
            edge(1)
        await_bytes(recv01.at[a], s01.at[a])
        pair = p01[a, 0] + recv01[a, 0]
        four = (p01[a, 1] + recv01[a, 1]) + (recv01[a, 2] + recv01[a, 3])
        await_bytes(recv_low.at[a], sg1.at[a])
        spread(list(range(2, 6)), [pair, four, tfull[a, 0, 0], tfull[a, 1, 0]])
        await_bytes(halo.at[a, 0], hs_send.at[a, 0])
        await_bytes(halo.at[a, 1], hs_send.at[a, 1])

    def top_levels(a, finish):
        await_bytes(recv_top.at[a], sg2.at[a])
        levels = [tfull[a, 0, 1], tfull[a, 1, 1], tfull[a, 0, 2], tfull[a, 1, 2]]
        pieces, rows = scaled_pieces(list(range(6, 10)), levels)
        for start in range(0, WIDTH, 512):
            span = slice(start, start + 512)
            q = finish(span, product(dot_nn, pieces, bh[rows, span], bl[rows, span]))
            qvec[:, span] = q
            fs[:, LEAF + start : LEAF + start + 512] = split3(q)

    def steps(total):
        norm, curve, cross, square = as_columns(total)
        step = norm / curve
        fresh = jnp.maximum(norm - 2.0 * step * cross + step * step * square, 0.0)
        return step, fresh / norm

    loads[0].wait()
    start = qvec[...]
    fs[:, LEAF : LEAF + WIDTH] = split3(start)
    sol_ref[...] = jnp.zeros_like(sol_ref)
    res_ref[...] = start
    dirn[...] = start
    apply(0, True)

    def first_image(span, top):
        image = zvec[:, span] + top
        wvec[:, span] = image
        return image

    top_levels(0, first_image)

    def iteration(a, carry):
        apply(a, False)
        step, ratio = steps(scalar_gather(a, 2, NY - 1, NC + NZ - 2))
        q = qvec[...]
        d = dirn[...]
        sol_ref[...] += step * d
        r = res_ref[...] - step * q
        res_ref[...] = r
        dirn[...] = r + ratio * d
        w = wvec[...] - step * zvec[...]
        wvec[...] = w
        qvec[...] = w + ratio * q

        def next_image(span, top):
            change = step * top
            wvec[:, span] -= change
            return qvec[:, span] - change

        top_levels(a, next_image)
        return carry

    lax.fori_loop(1, ITERS, iteration, 0)

    last = ITERS
    scs[last, 0] = dots_row()
    scalar_send(last, 0, cpeers, 0)
    scs[last, 1] = scalar_gather(last, 0, NC - 1, 0)
    scalar_send(last, 1, fpeers, NC - 1)
    step, _ = steps(scalar_gather(last, 1, len(FAR), NC - 1))
    sol_ref[...] += step * dirn[...]
    res_ref[...] += -step * qvec[...]

    def drain(a, carry):
        await_bytes(recv_top.at[a], s_top_send.at[a])
        await_bytes(recv_low.at[a], s_low_send.at[a])
        await_bytes(recv01.at[a], s01_send.at[a])
        await_bytes(recv_twin.at[a], s_twin_send.at[a])
        await_bytes(recv_z.at[a], s_z_send.at[a])
        await_bytes(recv_y.at[a], s_y_send.at[a])
        await_bytes(recv_low.at[a], sg1_send.at[a])
        await_bytes(recv_top.at[a], sg2_send.at[a])
        return carry

    def drain_scalars(a, carry):
        for phase, (base, count) in enumerate(((0, NC - 1), (NC - 1, NZ - 1), (NC + NZ - 2, NY - 1))):
            await_bytes(scr.at[a, pl.ds(base, count)], ssc_send.at[a, phase])
        return carry

    lax.fori_loop(0, ITERS, drain, 0)
    lax.fori_loop(1, ITERS, drain_scalars, 0)
    await_bytes(scr.at[last, pl.ds(0, NC - 1)], ssc_send.at[last, 0])
    await_bytes(scr.at[last, pl.ds(NC - 1, len(FAR))], ssc_send.at[last, 1])
    for side in range(2):
        await_bytes(chalo.at[side], cs_send.at[side])


def hand_over(sol_ref, res_ref, sol_out, res_out):
    sol_out[...] = sol_ref[...]
    res_out[...] = res_ref[...]


def per_device(rhs, coords, nugget, near_ids, basis):
    anywhere = pl.BlockSpec(memory_space=pl.ANY)
    vmem = pl.BlockSpec(memory_space=pltpu.VMEM)
    state = pltpu.VMEM((NRHS, WIDTH), F32)
    dma = pltpu.SemaphoreType.DMA
    n = ITERS
    scratch = [
        pltpu.VMEM((LEVELS, RANK, WIDTH), F32),
        pltpu.VMEM((LEVELS * RANK, WIDTH), BF16),
        pltpu.VMEM((LEVELS * RANK, WIDTH), BF16),
        pltpu.VMEM((LEAVES, 3 * LEAF, LEAF), BF16),
        pltpu.VMEM((LEAVES, 3 * LEAF, LEAF), BF16),
        pltpu.VMEM((3, WIDTH + 2 * LEAF), F32),
        pltpu.VMEM((1, WIDTH), F32),
        pltpu.VMEM((2, 3, LEAF), F32),
        pltpu.VMEM((3 * NRHS, WIDTH + 2 * LEAF), BF16),
        state,
        state,
        state,
        state,
        pltpu.VMEM((n, 2, NRHS, LEAF), F32),
        pltpu.VMEM((n, 2, 3, NRHS, RANK), F32),
        pltpu.VMEM((n, 2, NRHS, RANK), F32),
        pltpu.VMEM((n, NC - 1, 2, 8, RANK), F32),
        pltpu.VMEM((n, NC - 1, 8, RANK), F32),
        pltpu.VMEM((n, 4, NRHS, RANK), F32),
        pltpu.VMEM((n, 8, RANK), F32),
        pltpu.VMEM((n, 8, RANK), F32),
        pltpu.VMEM((n, NZ - 1, 2, 8, RANK), F32),
        pltpu.VMEM((n, 2, 8, RANK), F32),
        pltpu.VMEM((n, NZ * (NY - 1), 8, RANK), F32),
        pltpu.VMEM((n, 2, 3, NRHS, RANK), F32),
        pltpu.VMEM((n + 1, 3, 1, RANK), F32),
        pltpu.VMEM((n + 1, LINES, 1, RANK), F32),
        dma((LEVELS,)),
        dma((3,)),
        dma((2,)),
        dma((n, 2)),
        dma((n,)),
        dma((n,)),
        dma((n,)),
        dma((n,)),
        dma((n,)),
        dma((n,)),
        dma((n,)),
        dma((n,)),
        dma((n + 1, 3)),
        dma((2,)),
        dma((n, 2)),
        dma((n,)),
        dma((n,)),
        dma((n,)),
        dma((n,)),
        dma((n,)),
        dma((n,)),
        dma((n,)),
        dma((n,)),
        dma((n + 1, 3)),
    ]
    field = jax.ShapeDtypeStruct((NRHS, WIDTH), F32)
    parts = pl.pallas_call(
        kernel,
        out_shape=[field] * 2,
        in_specs=[anywhere, anywhere, anywhere, pl.BlockSpec(memory_space=pltpu.SMEM), anywhere],
        out_specs=[vmem, vmem],
        scratch_shapes=scratch,
        compiler_params=pltpu.CompilerParams(
            collective_id=0, has_side_effects=True, vmem_limit_bytes=56 * 1024 * 1024
        ),
    )(rhs, coords, nugget.reshape(1, WIDTH), near_ids, basis)
    return tuple(
        pl.pallas_call(
            hand_over,
            out_shape=[field] * 2,
            in_specs=[vmem] * 2,
            out_specs=[vmem] * 2,
        )(*parts)
    )


def solution(mesh):
    placed = (
        P(None, ("row", "col")),
        P(None, ("row", "col")),
        P(("row", "col")),
        P(("row", "col"), None),
        P(None, None, ("row", "col")),
    )
    return jax.shard_map(
        per_device,
        mesh=mesh,
        in_specs=placed,
        out_specs=(P(None, ("row", "col")), P(None, ("row", "col"))),
        check_vma=False,
    )
```

time: 115 us -> 98.4 us (0.86)
  Pallas kernels: 110 us -> 97.6 us
  local copies, waits for them, and re-layouts: 3.34 us -> 0 us
    pallas_call x1 -> x2, Pallas kernels: 110 us -> 97.6 us  [the longest x1 95.8 us: per_device(): pl.pallas_call(kernel, out_shape=[field] * 2, in_specs=[anywhere, anywher...]
    unnamed x2 -> x0, local copies, waits for them, and re-layouts: 3.34 us -> none
where the time goes in v2:
time: 98.4 us; the launch traced here: 98.3 us
  Pallas kernels  97.6 us (99%)
    pallas_call x1, Pallas kernels, per_device(): pl.pallas_call(kernel, out_shape=[field] * 2, in_specs=[anywhere, anywher...  95.8 us

profile of v2, /device:TPU:1, one launch (start us, length us, event | category | flops | bytes accessed | tf_op | source)
XLA Modules:
  0.0 98.3 jit_solution(15603597988340430473)
XLA Ops:
  0.6 95.8 %shard_map.68 = (f32[32,2048]{1,0:T(8,128)}, f32[32,2048]{1,0:T(8,128)}) custom-call(f32[32,2048]{1,0:T(8,128)} %rhs_hbm.1, f32[3,2048]{1,0:T(4,128)} %coords_hbm.1, f32[1,2048]{1,0:T(1,128)} %bitcast.1, s32[4,3]{1,0:T(4,128)} %ids_ref.1, f32[10,128,2048]{2,1,0:T(8,128)} %basis_ref.1), custom_call_target="tpu_custom_call" | custom-call | tf_op jit(solution)/shard_map/pallas_call | solution.py:575
  96.5 1.8 %shard_map.69 = (f32[32,2048]{1,0:T(8,128)}, f32[32,2048]{1,0:T(8,128)}) custom-call(f32[32,2048]{1,0:T(8,128)} %get-tuple-element.4.sol_ref, f32[32,2048]{1,0:T(8,128)} %get-tuple-element.5.res_ref), custom_call_target="tpu_custom_call" | custom-call | tf_op jit(solution)/shard_map/pallas_call | solution.py:586

commit v3 on v2

--- a/solution.py
+++ b/solution.py
@@ -30,10 +30,6 @@
     return lax.dot_general(a, b, (((1,), (0,)), ((), ())), preferred_element_type=F32)
 
 
-def dot_nt(a, b):
-    return lax.dot_general(a, b, (((1,), (1,)), ((), ())), preferred_element_type=F32)
-
-
 def thirds(value):
     first = value.astype(BF16)
     rest = value - first.astype(F32)
@@ -61,6 +57,8 @@
     [(j, k) for j in range(NY) for k in range(NZ) if j + k > 0],
     key=lambda jk: (-ring(jk[0], NY) - ring(jk[1], NZ), jk),
 )
+COL_ORDER = (4, 5, 3, 2, 6, 7, 1)
+Z_ORDER = (4, 3, 5, 2, 6, 1, 7)
 LINES = (NC - 1) + len(FAR)
 
 
@@ -75,6 +73,8 @@
     stage,
     bh,
     bl,
+    bth,
+    btl,
     th,
     tl,
     cext,
@@ -99,6 +99,7 @@
     tfull,
     scs,
     scr,
+    gate,
     bsem,
     isem,
     csem,
@@ -155,7 +156,7 @@
     loads[1].start()
     loads[2].start()
     barrier = pltpu.get_barrier_semaphore()
-    greeted = fpeers + cpeers + [left, right]
+    greeted = zpeers + cpeers + ypeers + [left, right]
     for peer in greeted:
         pl.semaphore_signal(barrier, inc=1, device_id=peer, device_id_type=MESH)
 
@@ -196,8 +197,9 @@
         )
 
     def scalar_send(a, phase, peers, base):
-        for k, peer in enumerate(peers):
-            send(scs.at[a, phase], scr.at[a, base + k], ssc_send.at[a, phase], ssc.at[a, phase], peer)
+        order = {NC - 1: COL_ORDER if phase == 0 else Z_ORDER}.get(len(peers), range(1, len(peers) + 1))
+        for k in order:
+            send(scs.at[a, phase], scr.at[a, base + k - 1], ssc_send.at[a, phase], ssc.at[a, phase], peers[k - 1])
 
     def scalar_gather(a, phase, count, base):
         await_bytes(scr.at[a, pl.ds(base, count)], ssc.at[a, phase])
@@ -209,18 +211,22 @@
     def load_levels(levels):
         for level in levels:
             pltpu.make_async_copy(basis_ref.at[level], stage.at[level], bsem.at[level]).wait()
+            rows = slice(level * RANK, (level + 1) * RANK)
             value = stage[level]
-            rows = slice(level * RANK, (level + 1) * RANK)
             high = value.astype(BF16)
             bh[rows, :] = high
             bl[rows, :] = (value - high.astype(F32)).astype(BF16)
+            value = jnp.transpose(stage[level])
+            high = value.astype(BF16)
+            bth[:, rows] = high
+            btl[:, rows] = (value - high.astype(F32)).astype(BF16)
 
     def own(start, width):
         return fs[:, LEAF + start : LEAF + start + width]
 
     def skeleton_pair(a, level):
         rows = slice(level * RANK, (level + 2) * RANK)
-        both = product(dot_nt, own(0, WIDTH), bh[rows, :], bl[rows, :])
+        both = product(dot_nn, own(0, WIDTH), bth[:, rows], btl[:, rows])
         for side in range(2):
             part = both[:, side * RANK : (side + 1) * RANK]
             if level == 2:
@@ -239,13 +245,14 @@
             zvec[:, span] += product(dot_nn, pieces, bh[rows, span], bl[rows, span])
 
     def local_levels():
-        for level, cluster in ((0, 2 * LEAF), (1, 4 * LEAF)):
-            rows = slice(level * RANK, (level + 1) * RANK)
-            for start in range(0, WIDTH, cluster):
-                span = slice(start, start + cluster)
-                skeleton = product(dot_nt, own(start, cluster), bh[rows, span], bl[rows, span])
-                pieces = split3(skeleton * (1.0 / cluster))
-                zvec[:, span] += product(dot_nn, pieces, bh[rows, span], bl[rows, span])
+        rows = slice(0, 2 * RANK)
+        half = WIDTH // 2
+        spans = [slice(0, half), slice(half, WIDTH)]
+        parts = [product(dot_nn, own(span.start, half), bth[span, rows], btl[span, rows]) for span in spans]
+        whole = (parts[0][:, RANK:] + parts[1][:, RANK:]) * (1.0 / WIDTH)
+        for span, part in zip(spans, parts):
+            pieces = split3(jnp.concatenate([part[:, :RANK] * (1.0 / half), whole], axis=1))
+            zvec[:, span] += product(dot_nn, pieces, bh[rows, span], bl[rows, span])
 
     def mask_value(leaf, offset):
         target = dev * LEAVES + leaf + offset - 1
@@ -302,22 +309,26 @@
 
     def apply(a, first):
         if first:
-            for level in (8, 6, 4, 2):
-                load_levels([level, level + 1])
-                skeleton_pair(a, level)
+            load_levels([8, 9, 6, 7])
+            skeleton_pair(a, 8)
+            skeleton_pair(a, 6)
             pl.semaphore_wait(barrier, len(greeted))
         else:
             skeleton_pair(a, 8)
             skeleton_pair(a, 6)
-        for k in range(1, NC):
+        for k in COL_ORDER:
             half, rows = eighth(k)
             part = prs.at[a, half, pl.ds(1, 2), rows, :]
             send(part, recv_top.at[a, k - 1], s_top_send.at[a], s_top.at[a], cpeers[k - 1])
-        if not first:
+        if first:
+            for peer in ypeers:
+                pl.semaphore_signal(gate, inc=1, device_id=peer, device_id_type=MESH)
+            load_levels([4, 5])
+        else:
             scs[a, 0] = dots_row()
             scalar_send(a, 0, cpeers, 0)
-            skeleton_pair(a, 4)
-        for k in range(1, NC):
+        skeleton_pair(a, 4)
+        for k in COL_ORDER:
             half, rows = eighth(k)
             send(prs.at[a, half, 0, rows, :], recv_low.at[a, k - 1], s_low_send.at[a], s_low.at[a], cpeers[k - 1])
         send(qvec.at[:, 0:LEAF], halo.at[a, 1], hs_send.at[a, 1], hsem.at[a, 1], left)
@@ -327,8 +338,8 @@
             loads[2].wait()
             send(cext.at[:, LEAF : 2 * LEAF], chalo.at[1], cs_send.at[1], csem.at[1], left)
             send(cext.at[:, WIDTH : WIDTH + LEAF], chalo.at[0], cs_send.at[0], csem.at[0], right)
-        else:
-            skeleton_pair(a, 2)
+            load_levels([2, 3])
+        skeleton_pair(a, 2)
         send(p01.at[a, 0], recv01.at[a, 0], s01_send.at[a], s01.at[a], core)
         for k in range(3):
             send(p01.at[a, 1], recv01.at[a, k + 1], s01_send.at[a], s01.at[a], quad[k])
@@ -354,6 +365,8 @@
             for k in range(NC - 1):
                 total = total + recv_top[a, k, t]
             ysend[a, t] = total
+        if first:
+            pl.semaphore_wait(gate, len(ypeers))
         for n, (j, k) in enumerate(FAR):
             if j == 0:
                 send(ysend.at[a], recv_z.at[a, k - 1], s_z_send.at[a], s_z.at[a], fpeers[n])
@@ -379,7 +392,7 @@
         await_bytes(recv_twin.at[a], s_twin.at[a])
         tfull[a, hh, 0, my_rows, :] = twin_send[a] + hh.astype(F32) * recv_twin[a]
         mine = tfull.at[a, hh, 0, my_rows, :]
-        for k in range(1, NC):
+        for k in COL_ORDER:
             send(mine, mine, sg1_send.at[a], sg1.at[a], cpeers[k - 1])
         if first:
             load_levels([0, 1])
@@ -407,7 +420,7 @@
         tfull[a, hh, 1, my_rows, :] = one
         tfull[a, hh, 2, my_rows, :] = two
         mine = tfull.at[a, hh, pl.ds(1, 2), my_rows, :]
-        for k in range(1, NC):
+        for k in COL_ORDER:
             send(mine, mine, sg2_send.at[a], sg2.at[a], cpeers[k - 1])
 
         if first:
@@ -522,6 +535,8 @@
         pltpu.VMEM((LEVELS, RANK, WIDTH), F32),
         pltpu.VMEM((LEVELS * RANK, WIDTH), BF16),
         pltpu.VMEM((LEVELS * RANK, WIDTH), BF16),
+        pltpu.VMEM((WIDTH, LEVELS * RANK), BF16),
+        pltpu.VMEM((WIDTH, LEVELS * RANK), BF16),
         pltpu.VMEM((LEAVES, 3 * LEAF, LEAF), BF16),
         pltpu.VMEM((LEAVES, 3 * LEAF, LEAF), BF16),
         pltpu.VMEM((3, WIDTH + 2 * LEAF), F32),
@@ -546,6 +561,7 @@
         pltpu.VMEM((n, 2, 3, NRHS, RANK), F32),
         pltpu.VMEM((n + 1, 3, 1, RANK), F32),
         pltpu.VMEM((n + 1, LINES, 1, RANK), F32),
+        pltpu.SemaphoreType.REGULAR,
         dma((LEVELS,)),
         dma((3,)),
         dma((2,)),

time: 98.4 us -> 93.2 us (0.947)
  Pallas kernels: 97.6 us -> 92.5 us
    pallas_call x1, Pallas kernels: 95.8 us -> 90.6 us  [per_device(): pl.pallas_call(kernel, out_shape=[field] * 2, in_specs=[anywhere, anywher...]
where the time goes in v3:
time: 93.2 us; the launch traced here: 93.1 us
  Pallas kernels  92.5 us (99%)
    pallas_call x1, Pallas kernels, per_device(): pl.pallas_call(kernel, out_shape=[field] * 2, in_specs=[anywhere, anywher...  90.6 us

profile of v3, /device:TPU:1, one launch (start us, length us, event | category | flops | bytes accessed | tf_op | source)
XLA Modules:
  0.0 93.1 jit_solution(7133890821616428816)
XLA Ops:
  0.6 90.6 %shard_map.68 = (f32[32,2048]{1,0:T(8,128)}, f32[32,2048]{1,0:T(8,128)}) custom-call(f32[32,2048]{1,0:T(8,128)} %rhs_hbm.1, f32[3,2048]{1,0:T(4,128)} %coords_hbm.1, f32[1,2048]{1,0:T(1,128)} %bitcast.1, s32[4,3]{1,0:T(4,128)} %ids_ref.1, f32[10,128,2048]{2,1,0:T(8,128)} %basis_ref.1), custom_call_target="tpu_custom_call" | custom-call | tf_op jit(solution)/shard_map/pallas_call | solution.py:591
  91.3 1.8 %shard_map.69 = (f32[32,2048]{1,0:T(8,128)}, f32[32,2048]{1,0:T(8,128)}) custom-call(f32[32,2048]{1,0:T(8,128)} %get-tuple-element.4.sol_ref, f32[32,2048]{1,0:T(8,128)} %get-tuple-element.5.res_ref), custom_call_target="tpu_custom_call" | custom-call | tf_op jit(solution)/shard_map/pallas_call | solution.py:602

commit v4 on v3

--- a/solution.py
+++ b/solution.py
@@ -97,6 +97,9 @@
     ysend,
     recv_y,
     tfull,
+    top_res,
+    top_dir,
+    wide,
     scs,
     scr,
     gate,
@@ -464,6 +467,13 @@
 
     top_levels(0, first_image)
 
+    def own_top(a, t):
+        return tfull[a, hh, t + 1, my_rows, :]
+
+    for t in range(2):
+        top_res[t] = own_top(0, t)
+        top_dir[t] = own_top(0, t)
+
     def iteration(a, carry):
         apply(a, False)
         step, ratio = steps(scalar_gather(a, 2, NY - 1, NC + NZ - 2))
@@ -477,6 +487,26 @@
         wvec[...] = w
         qvec[...] = w + ratio * q
 
+        wide[0] = jnp.broadcast_to(step, (NRHS, RANK))
+        wide[1] = jnp.broadcast_to(ratio, (NRHS, RANK))
+        step_rows = wide[0, my_rows, :]
+        ratio_rows = wide[1, my_rows, :]
+        for t in range(2):
+            top_res[t] = top_res[t] - step_rows * own_top(a, t)
+            top_dir[t] = top_res[t] + ratio_rows * top_dir[t]
+
+        @pl.when(a == ITERS - 1)
+        def _():
+            share = jnp.where(hh == 1, 0.25, 1.0).astype(F32) * 2.0**-18
+            part = top_dir[0] * own_top(a, 0) + (1.0 / 16.0) * (top_dir[1] * own_top(a, 1))
+            part = jnp.sum(part * step_rows, axis=1, keepdims=True) * share
+            wide[0] = jnp.zeros((NRHS, RANK), F32)
+            wide[0, my_rows, :] = jnp.broadcast_to(part, (8, RANK))
+            r = res_ref[...]
+            curve = jnp.sum(dirn[...] * qvec[...], axis=1, keepdims=True) - wide[0][:, 0:1]
+            scs[ITERS, 0] = as_row([jnp.sum(r * r, axis=1, keepdims=True), curve])
+            scalar_send(ITERS, 0, cpeers, 0)
+
         def next_image(span, top):
             change = step * top
             wvec[:, span] -= change
@@ -488,8 +518,6 @@
     lax.fori_loop(1, ITERS, iteration, 0)
 
     last = ITERS
-    scs[last, 0] = dots_row()
-    scalar_send(last, 0, cpeers, 0)
     scs[last, 1] = scalar_gather(last, 0, NC - 1, 0)
     scalar_send(last, 1, fpeers, NC - 1)
     step, _ = steps(scalar_gather(last, 1, len(FAR), NC - 1))
@@ -518,11 +546,6 @@
     await_bytes(scr.at[last, pl.ds(NC - 1, len(FAR))], ssc_send.at[last, 1])
     for side in range(2):
         await_bytes(chalo.at[side], cs_send.at[side])
-
-
-def hand_over(sol_ref, res_ref, sol_out, res_out):
-    sol_out[...] = sol_ref[...]
-    res_out[...] = res_ref[...]
 
 
 def per_device(rhs, coords, nugget, near_ids, basis):
@@ -559,6 +582,9 @@
         pltpu.VMEM((n, 2, 8, RANK), F32),
         pltpu.VMEM((n, NZ * (NY - 1), 8, RANK), F32),
         pltpu.VMEM((n, 2, 3, NRHS, RANK), F32),
+        pltpu.VMEM((2, 8, RANK), F32),
+        pltpu.VMEM((2, 8, RANK), F32),
+        pltpu.VMEM((2, NRHS, RANK), F32),
         pltpu.VMEM((n + 1, 3, 1, RANK), F32),
         pltpu.VMEM((n + 1, LINES, 1, RANK), F32),
         pltpu.SemaphoreType.REGULAR,
@@ -587,10 +613,9 @@
         dma((n,)),
         dma((n + 1, 3)),
     ]
-    field = jax.ShapeDtypeStruct((NRHS, WIDTH), F32)
     parts = pl.pallas_call(
         kernel,
-        out_shape=[field] * 2,
+        out_shape=[pltpu.VMEM((NRHS, WIDTH), F32)] * 2,
         in_specs=[anywhere, anywhere, anywhere, pl.BlockSpec(memory_space=pltpu.SMEM), anywhere],
         out_specs=[vmem, vmem],
         scratch_shapes=scratch,
@@ -598,14 +623,7 @@
             collective_id=0, has_side_effects=True, vmem_limit_bytes=56 * 1024 * 1024
         ),
     )(rhs, coords, nugget.reshape(1, WIDTH), near_ids, basis)
-    return tuple(
-        pl.pallas_call(
-            hand_over,
-            out_shape=[field] * 2,
-            in_specs=[vmem] * 2,
-            out_specs=[vmem] * 2,
-        )(*parts)
-    )
+    return tuple(parts)
 
 
 def solution(mesh):

time: 93.2 us -> 91 us (0.976)
  Pallas kernels: 92.5 us -> 88.9 us
  local copies, waits for them, and re-layouts: 0 us -> 1.41 us
    pallas_call x2 -> x1, Pallas kernels: 92.5 us -> 88.9 us  [per_device(): pl.pallas_call(kernel, out_shape=[pltpu.VMEM((NRHS, WIDTH), F32)] * 2, in...]
    unnamed x0 -> x2, local copies, waits for them, and re-layouts: none -> 1.41 us
where the time goes in v4:
time: 91 us; the launch traced here: 90.9 us
  Pallas kernels  88.9 us (98%)
  local copies, waits for them, and re-layouts  1.41 us (2%)
    pallas_call x1, Pallas kernels, per_device(): pl.pallas_call(kernel, out_shape=[pltpu.VMEM((NRHS, WIDTH), F32)] * 2, in...  88.9 us

profile of v4, /device:TPU:1, one launch (start us, length us, event | category | flops | bytes accessed | tf_op | source)
XLA Modules:
  0.0 90.9 jit_solution(7024292601599066384)
XLA Ops:
  0.6 88.9 %shard_map.68 = (f32[32,2048]{1,0:T(8,128)S(1)}, f32[32,2048]{1,0:T(8,128)S(1)}) custom-call(f32[32,2048]{1,0:T(8,128)} %rhs_hbm.1, f32[3,2048]{1,0:T(4,128)} %coords_hbm.1, f32[1,2048]{1,0:T(1,128)} %bitcast.1, s32[4,3]{1,0:T(4,128)} %ids_ref.1, f32[10,128,2048]{2,1,0:T(8,128)} %basis_ref.1), custom_call_target="tpu_custom_call" | custom-call | tf_op jit(solution)/shard_map/pallas_call | solution.py:616
  89.5 0.7 copy.9
  90.2 0.7 copy.10

commit v5 on v4

--- a/solution.py
+++ b/solution.py
@@ -153,15 +153,19 @@
         pltpu.make_async_copy(coords_hbm, cext.at[:, LEAF : LEAF + WIDTH], isem.at[1]),
         pltpu.make_async_copy(nugget_hbm, nugget_ref, isem.at[2]),
     ]
+    def fetch(levels):
+        for level in levels:
+            pltpu.make_async_copy(basis_ref.at[level], stage.at[level], bsem.at[level]).start()
+
     loads[0].start()
-    for level in (8, 9, 6, 7, 4, 5, 2, 3, 0, 1):
-        pltpu.make_async_copy(basis_ref.at[level], stage.at[level], bsem.at[level]).start()
+    fetch((8, 9, 6, 7))
+    barrier = pltpu.get_barrier_semaphore()
+    greeted = [zpeers[k - 1] for k in Z_ORDER] + ypeers + [left, right] + [cpeers[k - 1] for k in COL_ORDER]
+    for peer in greeted:
+        pl.semaphore_signal(barrier, inc=1, device_id=peer, device_id_type=MESH)
+    fetch((4, 5, 2, 3, 0, 1))
     loads[1].start()
     loads[2].start()
-    barrier = pltpu.get_barrier_semaphore()
-    greeted = zpeers + cpeers + ypeers + [left, right]
-    for peer in greeted:
-        pl.semaphore_signal(barrier, inc=1, device_id=peer, device_id_type=MESH)
 
     def send(src, dst, send_sem, recv_sem, peer):
         pltpu.make_async_remote_copy(

time: 91 us -> 90.3 us (level)
  no operation moved by 1% of the time
where the time goes in v5:
time: 90.3 us; the launch traced here: 90.1 us
  Pallas kernels  88.1 us (98%)
  local copies, waits for them, and re-layouts  1.41 us (2%)
    pallas_call x1, Pallas kernels, per_device(): pl.pallas_call(kernel, out_shape=[pltpu.VMEM((NRHS, WIDTH), F32)] * 2, in...  88.1 us

profile of v5, /device:TPU:1, one launch (start us, length us, event | category | flops | bytes accessed | tf_op | source)
XLA Modules:
  0.0 90.1 jit_solution(14991000736471393750)
XLA Ops:
  0.6 88.1 %shard_map.68 = (f32[32,2048]{1,0:T(8,128)S(1)}, f32[32,2048]{1,0:T(8,128)S(1)}) custom-call(f32[32,2048]{1,0:T(8,128)} %rhs_hbm.1, f32[3,2048]{1,0:T(4,128)} %coords_hbm.1, f32[1,2048]{1,0:T(1,128)} %bitcast.1, s32[4,3]{1,0:T(4,128)} %ids_ref.1, f32[10,128,2048]{2,1,0:T(8,128)} %basis_ref.1), custom_call_target="tpu_custom_call" | custom-call | tf_op jit(solution)/shard_map/pallas_call | solution.py:620
  88.7 0.7 copy.9
  89.4 0.7 copy.10
